TPU v7x, 32 devices: a whole 2x2x4 slice. The times are simulated.
32 devices in a mesh: sub: 8 (over z, core), mem: 4 (over y, x).
Axes of the slice: x: 2, y: 2, z: 4, core: 2. Of those that a mesh axis runs over, the one named last changes fastest.
Arguments:
- dechirped_echo_matrix: bfloat16 [8, 2, 256, 8192], P('sub', None, 'mem'), may hold values from -6 to 6
- bearing_rotation_table: float32 [8, 4, 512, 256], P('sub', 'mem'), may hold values from -3.140625 to 3.140625
- patch_subset_holder: int32 [8, 4, 64], P('sub', 'mem'), may hold values from 0 to 7, as said below
- modulation_slope: float32 [8, 4, 2, 64], P('sub', 'mem'), may hold values from -0.5 to 0.5
- regrid_lead_cell: int32 [8, 4, 2, 128], P('sub', 'mem'), may hold values from 0 to 124
- regrid_weight: float32 [8, 4, 2, 128], P('sub', 'mem'), may hold values from 0 to 1
Outputs:
- ground_image: bfloat16 [32, 2, 128, 128], P(('sub', 'mem'))
Inputs may be any that keep to these rules, and one draw needn't show every extreme that they name: `patch_subset_holder`: each group and sector sends at most 16 of its 64 blocks to any one tile; in every sector some tile receives exactly 16 blocks from every group.
All inputs are finite; a program needn't handle non-finite values.
Results may differ from a plain program's by a relative error of at most 0.014.
Values may be sent and summed in bfloat16 or wider, within the bound.
A program may use at most 64 MiB of HBM per device.

v0:
```python
import math

import jax
import jax.numpy as jnp
from jax import lax
from jax.sharding import PartitionSpec as P

FREQUENCIES = 8192
FIRST_RADIX = 64
SECOND_RADIX = 128
SWEEPS = 256
ANGLES = 512
BLOCK_SIDE = 128


def dft_tables(length):
    positions = jnp.arange(length, dtype=jnp.int32)
    turns = positions[:, None] * positions[None, :] % length
    phase_angle = turns.astype(jnp.float32) * (2.0 * math.pi / length)
    return jnp.stack([jnp.cos(phase_angle), jnp.sin(phase_angle)]).astype(jnp.bfloat16)


def twiddle(row_count, column_count, length):
    row_index = jnp.arange(row_count, dtype=jnp.int32)
    column_index = jnp.arange(column_count, dtype=jnp.int32)
    turns = row_index[:, None] * column_index[None, :] % length
    phase_angle = turns.astype(jnp.float32) * (2.0 * math.pi / length)
    return (jnp.cos(phase_angle), jnp.sin(phase_angle))


def combine(product):
    return (product[0, 0] - product[1, 1], product[0, 1] + product[1, 0])


def range_transform(sweeps):
    sweep_count = sweeps.shape[1]
    reshaped = sweeps.reshape(2, sweep_count, FIRST_RADIX, SECOND_RADIX)
    product = jnp.einsum(
        "qrk,pskj->qpsrj", dft_tables(FIRST_RADIX), reshaped, preferred_element_type=jnp.float32
    )
    inphase_part, quadrature_part = combine(product)
    cosine, sine_part = twiddle(FIRST_RADIX, SECOND_RADIX, FREQUENCIES)
    turned = jnp.stack(
        [
            inphase_part * cosine - quadrature_part * sine_part,
            inphase_part * sine_part + quadrature_part * cosine,
        ]
    ).astype(jnp.bfloat16)
    product = jnp.einsum(
        "quj,psrj->qpsur", dft_tables(SECOND_RADIX), turned, preferred_element_type=jnp.float32
    )
    inphase_part, quadrature_part = combine(product)
    factor = 1.0 / math.sqrt(FREQUENCIES)
    return (
        (jnp.stack([inphase_part, quadrature_part]) * factor)
        .astype(jnp.bfloat16)
        .reshape(2, sweep_count, FREQUENCIES)
    )


def phase_tables(angles):
    factor = 1.0 / math.sqrt(SWEEPS)
    return jnp.stack([jnp.cos(angles) * factor, jnp.sin(angles) * factor]).astype(jnp.bfloat16)


def strip_modulation(
    inphase_part, quadrature_part, modulation_line_entries, tilt_patches, slant_patches
):
    tilt_linear_slope = modulation_line_entries[0].reshape(tilt_patches, slant_patches)
    slant_linear_slope = modulation_line_entries[1].reshape(tilt_patches, slant_patches)
    positions = jnp.arange(BLOCK_SIDE, dtype=jnp.float32)
    phase_angle = (
        tilt_linear_slope[:, None, :, None] * positions[None, :, None, None]
        + slant_linear_slope[:, None, :, None] * positions[None, None, None, :]
    )
    cosine = jnp.cos(phase_angle)
    sine_part = jnp.sin(phase_angle)
    inphase_part = inphase_part.reshape(tilt_patches, BLOCK_SIDE, slant_patches, BLOCK_SIDE)
    quadrature_part = quadrature_part.reshape(tilt_patches, BLOCK_SIDE, slant_patches, BLOCK_SIDE)
    return jnp.stack(
        [
            inphase_part * cosine - quadrature_part * sine_part,
            inphase_part * sine_part + quadrature_part * cosine,
        ]
    ).astype(jnp.bfloat16)


def stencil(offsets, fractions):
    weights = [
        -fractions * (fractions - 1.0) * (fractions - 2.0) / 6.0,
        (fractions + 1.0) * (fractions - 1.0) * (fractions - 2.0) / 2.0,
        -(fractions + 1.0) * fractions * (fractions - 2.0) / 2.0,
        (fractions + 1.0) * fractions * (fractions - 1.0) / 6.0,
    ]
    sources = jnp.arange(fractions.shape[-1], dtype=jnp.int32)
    distance = sources - offsets[..., None]
    weights_sum = jnp.zeros(distance.shape, jnp.float32)
    for stencil_tap in range(4):
        weights_sum = weights_sum + jnp.where(
            distance == stencil_tap, weights[stencil_tap][..., None], jnp.float32(0.0)
        )
    return weights_sum.astype(jnp.bfloat16)


def on_device(
    dechirped_echo_matrix,
    bearing_rotation_table,
    patch_subset_holder,
    modulation_slope,
    regrid_lead_cell,
    regrid_weight,
):
    groups = lax.axis_size("sub")
    members = lax.axis_size("mem")
    sector = FREQUENCIES // members
    tilt_patches = ANGLES // BLOCK_SIDE
    slant_patches = sector // BLOCK_SIDE
    spectrum = range_transform(dechirped_echo_matrix[0])
    sweep_count = spectrum.shape[1]
    by_sector = spectrum.reshape(2, sweep_count, members, sector)
    tables = phase_tables(bearing_rotation_table[0, 0])
    product = jnp.einsum(
        "qas,psc->qpac",
        tables,
        lax.all_to_all(by_sector, "mem", split_axis=2, concat_axis=1, tiled=True)[:, :, 0, :],
        preferred_element_type=jnp.float32,
    )
    inphase_part, quadrature_part = combine(product)
    focused_image = jnp.stack([inphase_part, quadrature_part])[:, :, None, :]
    patch_list = strip_modulation(
        focused_image[0, :, 0, :],
        focused_image[1, :, 0, :],
        modulation_slope[0, 0],
        tilt_patches,
        slant_patches,
    )
    own_tables = stencil(regrid_lead_cell[0, 0], regrid_weight[0, 0])
    owners = patch_subset_holder[0, 0]
    onehot = owners[:, None] == jnp.arange(groups, dtype=jnp.int32)[None, :]
    all_tables = lax.all_gather(own_tables[None], "sub", axis=0, tiled=True)
    picker = onehot.astype(jnp.bfloat16).reshape(tilt_patches, slant_patches, groups)
    chosen = jnp.einsum(
        "ACo,odyx->ACdyx", picker, all_tables, preferred_element_type=jnp.float32
    ).astype(jnp.bfloat16)
    rows_done = jnp.einsum(
        "ACya,pAaCc->ACpyc", chosen[:, :, 0], patch_list, preferred_element_type=jnp.float32
    ).astype(jnp.bfloat16)
    interpolated = jnp.einsum(
        "ACpyc,ACxc->ACpyx", rows_done, chosen[:, :, 1], preferred_element_type=jnp.float32
    )
    contributions = jnp.einsum(
        "ACo,ACpyx->opyx", picker.astype(jnp.float32), interpolated, precision=lax.Precision.HIGHEST
    )
    ground = lax.psum_scatter(
        contributions.astype(jnp.bfloat16), "sub", scatter_dimension=0, tiled=True
    ).astype(jnp.float32)[0]
    return (0.25 * ground).astype(jnp.bfloat16)[None]


def solution(mesh):
    return jax.shard_map(
        on_device,
        mesh=mesh,
        in_specs=(
            P("sub", None, "mem", None),
            P("sub", "mem", None, None),
            P("sub", "mem", None),
            P("sub", "mem", None, None),
            P("sub", "mem", None, None),
            P("sub", "mem", None, None),
        ),
        out_specs=P(("sub", "mem"), None, None, None),
        check_vma=False,
    )
```

profile of v0, /device:TPU:0, one launch (start us, length us, event | category | flops | bytes accessed | tf_op | source)
XLA Modules:
  0.0 180.2 jit_solution(11648283646185296107)
XLA Ops:
  6.5 0.2 sine_convert_fusion.1
  6.7 0.1 fusion.67
  6.8 0.3 sine_convert_fusion
  7.1 2.2 %copy.65 = bf16[16,8,64,128]{3,2,1,0:T(8,128)(2,1)S(1)} copy(bf16[16,8,64,128]{3,1,2,0:T(8,128)(2,1)} %bitcast.125) | data formatting | bytes 4194304
  9.3 1.2 convolution_bitcast_fusion.1
  10.6 1.1 subtract_convert_fusion
  11.7 1.2 convolution_bitcast_fusion.2
  12.9 2.3 %slice_subtract_fusion.1 = (f32[1,1,64,128,64]{3,4,0,2,1:T(8,128)S(1)}, f32[1,1,64,128,64]{3,4,0,2,1:T(8,128)}) fusion(f32[2,2,64,128,64]{3,4,0,2,1:T(8,128)S(1)} %convolution_bitcast_fusion.2), kind=kLoop, calls=%fused_computation.30 | loop fusion | flops 1048576 | bytes 12582912 | tf_op jit(solution)/shard_map/sub | solution.py:32
  15.2 2.7 %copy.32 = f32[1,1,64,128,64]{4,3,2,1,0:T(8,128)} copy(f32[1,1,64,128,64]{3,4,0,2,1:T(8,128)S(1)} %get-tuple-element.13) | data formatting | bytes 4194304 | tf_op jit(solution)/shard_map/sub | solution.py:32
  17.9 5.2 %sub.105 = f32[1,64,4,2048]{3,2,1,0:T(4,128)} reshape(f32[1,1,64,128,64]{4,3,2,1,0:T(8,128)} %copy.32) | data formatting | bytes 4194304 | tf_op jit(solution)/shard_map/sub | solution.py:32
  23.1 2.8 %copy.34 = f32[1,64,4,2048]{3,1,2,0:T(8,128)S(1)} copy(f32[1,64,4,2048]{3,2,1,0:T(4,128)} %sub.105) | data formatting | bytes 4194304 | tf_op jit(solution)/shard_map/sub | solution.py:32
  25.9 3.8 %copy.33 = f32[1,1,64,128,64]{4,3,2,1,0:T(8,128)} copy(f32[1,1,64,128,64]{3,4,0,2,1:T(8,128)} %get-tuple-element.14) | data formatting | bytes 4194304 | tf_op jit(solution)/shard_map/add | solution.py:32
  29.7 5.1 %add.226 = f32[1,64,4,2048]{3,2,1,0:T(4,128)} reshape(f32[1,1,64,128,64]{4,3,2,1,0:T(8,128)} %copy.33) | data formatting | bytes 4194304 | tf_op jit(solution)/shard_map/add | solution.py:32
  34.8 2.8 %copy.35 = f32[1,64,4,2048]{3,1,2,0:T(8,128)S(1)} copy(f32[1,64,4,2048]{3,2,1,0:T(4,128)} %add.226) | data formatting | bytes 4194304 | tf_op jit(solution)/shard_map/add | solution.py:32
  37.6 0.5 fusion.10
  38.1 1.5 copy.36
  39.6 0.0 copy-start.4
  39.6 0.0 copy-start.5
  39.6 0.0 copy-start.3
  39.6 0.0 copy-start.2
  39.6 0.0 copy-start.1
  39.6 5.3 %all-to-all-start = ((bf16[2,64,4,2048]{3,1,0,2:T(8,128)(2,1)}), bf16[2,64,4,2048]{3,1,0,2:T(8,128)(2,1)S(1)}, u32[]{:S(2)}, u32[]{:S(2)}) async-start(bf16[2,64,4,2048]{3,1,0,2:T(8,128)(2,1)} %copy.36), calls=%async_computation | async-start | bytes 4194304 | tf_op jit(solution)/shard_map/all_to_all | solution.py:125
  44.9 0.0 reduce-scatter.2.cloned.1.call-start
  44.9 0.0 copy-done.4
  44.9 0.1 mul.422
  45.0 0.1 iota_multiply_fusion
  45.1 0.1 mul.418
  45.2 0.1 iota_multiply_fusion.1
  45.3 0.5 broadcast.516
  45.8 0.0 copy-done.5
  45.8 0.7 reduce.11
  46.4 0.1 eq.74
  46.5 0.0 copy-done.3
  46.5 0.0 copy-done.2
  46.5 0.2 add_convert_fusion.1
  46.8 15.3 %all_gather.3 = bf16[8,2,128,128]{3,2,1,0:T(8,128)(2,1)S(1)} all-gather(bf16[1,2,128,128]{3,2,1,0:T(8,128)(2,1)S(1)} %add_convert_fusion.1), channel_id=1, replica_groups=mesh['sub'=8,'mem'=4] {'sub'}, dimensions={0}, use_global_device_ids=true | all-gather | bytes 589824 | tf_op jit(solution)/shard_map/all_gather | solution.py:140
  62.1 0.0 copy-done.1
  62.1 1.9 %fusion.39 = (bf16[1,512,256]{2,1,0:T(8,128)(2,1)S(1)}, bf16[1,512,256]{2,1,0:T(8,128)(2,1)S(1)}) fusion(f32[1,1,512,256]{3,2,1,0:T(8,128)S(1)} %copy-done.1), kind=kLoop, calls=%fused_computation.51 | loop fusion | flops 524288 | bytes 1048576 | tf_op jit(solution)/shard_map/mul | solution.py:63
  64.0 1.5 convolution_convert_fusion
  65.5 2.7 %slice_bitcast_fusion.1 = (bf16[4,16,128,128,1]{3,1,2,0,4:T(8,128)(2,1)}, bf16[4,16,128,128,1]{3,1,2,0,4:T(8,128)(2,1)}) fusion(bf16[4,16,2,128,128]{4,1,3,2,0:T(8,128)(2,1)S(1)} %convolution_convert_fusion), kind=kLoop, calls=%fused_computation.28 | loop fusion | bytes 8388608 | tf_op jit(solution)/shard_map/squeeze | solution.py:146
  68.2 1.6 all-to-all-done
  69.8 0.1 copy.37
  69.9 8.2 %convolution_bitcast_fusion = f32[2,2,512,2048]{2,3,0,1:T(8,128)} fusion(bf16[2,256,2048,1]{2,1,3,0:T(8,128)(2,1)S(1)} %bitcast.123, bf16[1,512,256]{2,1,0:T(8,128)(2,1)S(1)} %get-tuple-element.18, bf16[1,512,256]{2,1,0:T(8,128)(2,1)S(1)} %get-tuple-element.17), kind=kOutput, calls=%fused_computation.2 | convolution fusion | flops 2148532224 | bytes 19398656 | tf_op jit(solution)/shard_map/qas,psc->qpac/dot_general | solution.py:122
  78.1 11.2 %slice_subtract_fusion = (f32[1,1,512,2048]{2,3,0,1:T(8,128)}, f32[1,1,512,2048]{2,3,0,1:T(8,128)}) fusion(f32[2,2,512,2048]{2,3,0,1:T(8,128)} %convolution_bitcast_fusion), kind=kLoop, calls=%fused_computation.14 | loop fusion | flops 2097152 | bytes 25165824 | tf_op jit(solution)/shard_map/sub | solution.py:32
  89.2 5.2 %add.231 = f32[1,4,128,16,128]{2,1,4,3,0:T(4,128)} reshape(f32[1,1,512,2048]{2,3,0,1:T(8,128)} %get-tuple-element.8) | data formatting | bytes 8388608 | tf_op jit(solution)/shard_map/add | solution.py:32
  94.5 5.3 %sub.107 = f32[1,4,128,16,128]{2,1,4,3,0:T(4,128)} reshape(f32[1,1,512,2048]{2,3,0,1:T(8,128)} %get-tuple-element.7) | data formatting | bytes 8388608 | tf_op jit(solution)/shard_map/sub | solution.py:32
  99.8 0.0 copy-start
  99.8 19.2 %fusion.7 = (bf16[1,4,128,16,128]{2,4,0,3,1:T(8,128)(2,1)}, bf16[1,4,128,16,128]{2,4,0,3,1:T(8,128)(2,1)}) fusion(f32[1,4,128,16,128]{2,1,4,3,0:T(4,128)} %add.231, f32[1,4,128,16,128]{2,1,4,3,0:T(4,128)} %sub.107, f32[4,16,128]{2,1,0:T(8,128)S(1)} %iota_multiply_fusion, f32[4,128,16]{1,2,0:T(8,128)S(1)} %iota_multiply_fusion.1), kind=kLoop, calls=%fused_computation.10 | loop fusion | flops 9437184 | bytes 12648448 | tf_op jit(solution)/shard_map/convert
  119.0 0.0 copy-done
  119.0 8.5 %fusion.15 = f32[4,16,2,128,128]{4,3,2,1,0:T(8,128)} fusion(bf16[1,4,128,16,128]{2,4,0,3,1:T(8,128)(2,1)} %get-tuple-element.10, bf16[1,4,128,16,128]{2,4,0,3,1:T(8,128)(2,1)} %get-tuple-element.9, bf16[4,16,128,128,1]{3,1,2,0,4:T(8,128)(2,1)} %get-tuple-element.16, bf16[4,16,128,128,1]{3,1,2,0,4:T(8,128)(2,1)S(1)} %copy-done), kind=kOutput, calls=%fused_computation.21 | convolution fusion | flops 1077936128 | bytes 16777216 | tf_op jit(solution)/shard_map/ACpyc,ACxc->ACpyx/dot_general | solution.py:148
  127.5 11.9 %fusion.32 = bf16[8,2,128,128]{3,0,2,1:T(8,128)(2,1)S(1)} fusion(f32[4,16,2,128,128]{4,3,2,1,0:T(8,128)} %fusion.15, s32[4,16]{1,0:T(4,128)S(1)} %eq.74), kind=kOutput, calls=%fused_computation.43 | convolution fusion | flops 201589248 | bytes 8913152 | tf_op jit(solution)/shard_map/ACo,ACpyx->opyx/dot_general | solution.py:151
  139.4 0.9 copy.48
  140.3 0.0 reduce-scatter.2.cloned.1.call-update
  140.3 31.5 %reduce-scatter.2.cloned.1.call-done = bf16[1,2,128,128]{3,2,1,0:T(8,128)(2,1)} async-done(((bf16[8,2,128,128]{3,2,1,0:T(8,128)(2,1)}), bf16[1,2,128,128]{3,2,1,0:T(8,128)(2,1)}) %reduce-scatter.2.cloned.1.call-update) | async-done | bytes 65552 | tf_op jit(solution)/shard_map/reduce_scatter | solution.py:154
  171.8 1.5 multiply_convert_fusion.2
  (2 shorter events, 0.0 us)
Async XLA Ops:
  39.6 5.3 %copy-start.4 = (f32[1,1,2,64]{3,2,1,0:T(2,128)S(1)}, f32[1,1,2,64]{3,2,1,0:T(2,128)}, u32[]{:S(2)}) copy-start(f32[1,1,2,64]{3,2,1,0:T(2,128)} %param.9) | copy-start | bytes 1540
  39.6 6.2 %copy-start.5 = (s32[1,1,64]{2,1,0:T(1,128)S(1)}, s32[1,1,64]{2,1,0:T(1,128)}, u32[]{:S(2)}) copy-start(s32[1,1,64]{2,1,0:T(1,128)} %param.8) | copy-start | bytes 772
  39.6 7.0 %copy-start.3 = (f32[1,1,2,128]{3,2,1,0:T(2,128)S(1)}, f32[1,1,2,128]{3,2,1,0:T(2,128)}, u32[]{:S(2)}) copy-start(f32[1,1,2,128]{3,2,1,0:T(2,128)} %param.11) | copy-start | bytes 3076
  39.6 7.0 %copy-start.2 = (s32[1,1,2,128]{3,2,1,0:T(2,128)S(1)}, s32[1,1,2,128]{3,2,1,0:T(2,128)}, u32[]{:S(2)}) copy-start(s32[1,1,2,128]{3,2,1,0:T(2,128)} %param.10) | copy-start | bytes 3076
  39.6 22.5 %copy-start.1 = (f32[1,1,512,256]{3,2,1,0:T(8,128)S(1)}, f32[1,1,512,256]{3,2,1,0:T(8,128)}, u32[]{:S(2)}) copy-start(f32[1,1,512,256]{3,2,1,0:T(8,128)} %param.7) | copy-start | bytes 1572868
  39.6 30.2 %all-to-all-start = ((bf16[2,64,4,2048]{3,1,0,2:T(8,128)(2,1)}), bf16[2,64,4,2048]{3,1,0,2:T(8,128)(2,1)S(1)}, u32[]{:S(2)}, u32[]{:S(2)}) async-start(bf16[2,64,4,2048]{3,1,0,2:T(8,128)(2,1)} %copy.36), calls=%async_computation | async-start | bytes 4194304 | tf_op jit(solution)/shard_map/all_to_all | solution.py:125
  44.9 126.9 %reduce-scatter.2.cloned.1.call-start = ((), (), s32[]{:S(2)}) async-start(), calls=%async_computation.2 | async-start | bytes 589824 | tf_op jit(solution)/shard_map/reduce_scatter | solution.py:154
  99.8 19.3 %copy-start = (bf16[4,16,128,128,1]{3,1,2,0,4:T(8,128)(2,1)S(1)}, bf16[4,16,128,128,1]{3,1,2,0,4:T(8,128)(2,1)}, u32[]{:S(2)}) copy-start(bf16[4,16,128,128,1]{3,1,2,0,4:T(8,128)(2,1)} %get-tuple-element.15) | copy-start | bytes 6291460
Sparse Core Ops, SparseCore 0:
  140.5 31.3 reduce-scatter.1
where the time goes:
time: 181 us; the launch traced here: 180 us
  local copies, waits for them, and re-layouts  41.1 us (23%)
  other arithmetic  39.3 us (22%)
  waiting for transfers between devices  33.1 us (18%)
  matrix products  32.6 us (18%)
  blocking collectives  15.3 us (8%)
  between operations  13.5 us (7%)
  starting transfers between devices  5.32 us (3%)
    reduce_scatter x1, waiting for transfers between devices, on_device(): lax.psum_scatter(contributions.astype(jnp.bfloat16), 'sub', scatter_dimen...  31.5 us
    another operation x4, other arithmetic  20.8 us
    add x4, local copies, waits for them, and re-layouts, combine(): return (product[0, 0] - product[1, 1], product[0, 1] + product[1, 0])  17 us
    sub x4, local copies, waits for them, and re-layouts, combine(): return (product[0, 0] - product[1, 1], product[0, 1] + product[1, 0])  16 us
    all_gather x1, blocking collectives, on_device(): all_tables = lax.all_gather(own_tables[None], 'sub', axis=0, tiled=True)  15.3 us
    sub x2, other arithmetic, combine(): return (product[0, 0] - product[1, 1], product[0, 1] + product[1, 0])  13.4 us
    dot_general x1, matrix products, on_device(): jnp.einsum('ACo,ACpyx->opyx', picker.astype(jnp.float32), interpolated, p...  11.9 us
    dot_general x1, matrix products, on_device(): jnp.einsum('ACpyc,ACxc->ACpyx', rows_done, chosen[:, :, 1], preferred_ele...  8.48 us
  transfers between devices with their start and end apart: 2, of which 2 were waited for; matrix products, arithmetic and copies ran while one was open for 4% of the time, Pallas kernels for 0%

commit v1 on v0

v1 whole, which is shorter than its diff:
```python
import functools
import math

import jax
import jax.numpy as jnp
import ml_dtypes
import numpy as np
from jax import lax
from jax.experimental import pallas as pl
from jax.experimental.pallas import tpu as pltpu
from jax.sharding import PartitionSpec as P

SIDE = 128
F32 = jnp.float32
BF16 = jnp.bfloat16
VMEM_LIMIT = 48 * 1024 * 1024


def transform_tables(frequencies):
    coarse = frequencies // SIDE
    k2 = np.arange(coarse)
    k1 = np.arange(SIDE)
    first = 2.0 * np.pi * ((k2[:, None] * k2[None, :]) % coarse) / coarse
    second = 2.0 * np.pi * ((k2[:, None] * k1[None, :]) % coarse) / coarse
    turn = 2.0 * np.pi * (k1[:, None] * k1[None, :]) / frequencies

    def block(angle):
        c, s = np.cos(angle), np.sin(angle)
        return np.block([[c, -s], [s, c]]).astype(ml_dtypes.bfloat16)

    scale = 1.0 / math.sqrt(frequencies)
    turning = np.stack([np.cos(turn), np.sin(turn)]) * scale
    return block(first), block(second), turning.astype(np.float32)


def cos_sin(x):
    q = jnp.floor(x * (2.0 / math.pi) + 0.5)
    r = x - q * 1.5703125
    r = r - q * 4.837512969970703e-4
    r = r - q * 7.549789948768648e-8
    z = r * r
    s = r + r * z * (-1.6666654611e-1 + z * (8.3321608736e-3 + z * -1.9515295891e-4))
    c = 1.0 - 0.5 * z + z * z * (4.166664568298827e-2 + z * (-1.388731625493765e-3 + z * 2.443315711809948e-5))
    n = q.astype(jnp.int32)
    odd = (n & 1) == 1
    cos_base = jnp.where(odd, s, c)
    sin_base = jnp.where(odd, c, s)
    cos_neg = ((n + 1) & 2) == 2
    sin_neg = (n & 2) == 2
    return jnp.where(cos_neg, -cos_base, cos_base), jnp.where(sin_neg, -sin_base, sin_base)


def transform_kernel(x_ref, w1_ref, w2_ref, turn_ref, out_ref, xs, ys):
    sweeps = x_ref.shape[1]
    coarse = x_ref.shape[2] // SIDE
    members = out_ref.shape[0]
    bands = out_ref.shape[2]

    def spread(k2, carry):
        lanes = pl.ds(pl.multiple_of(k2 * SIDE, SIDE), SIDE)
        for p in range(2):
            rows = pl.ds(pl.multiple_of((p * coarse + k2) * sweeps, 16), sweeps)
            xs[rows, :] = x_ref[p, :, lanes].astype(F32)
        return carry

    lax.fori_loop(0, coarse, spread, 0, unroll=8)

    batch = 8

    def transform(step, carry):
        w1 = w1_ref[...]
        w2 = w2_ref[...]
        for j in range(batch):
            s = step * batch + j
            x = xs[pl.ds(s, 2 * coarse, stride=sweeps), :].astype(BF16)
            f = jnp.dot(w1, x, preferred_element_type=F32)
            re = jnp.concatenate([f[:coarse], f[:coarse]], axis=0)
            im = jnp.concatenate([f[coarse:], f[coarse:]], axis=0)
            cosine, sine = turn_ref[0], turn_ref[1]
            turned = jnp.concatenate(
                [(re * cosine - im * sine).astype(BF16), (re * sine + im * cosine).astype(BF16)], axis=1
            )
            y = lax.dot_general(w2, turned, (((1,), (1,)), ((), ())), preferred_element_type=F32)
            ys[pl.ds(s, 2 * coarse, stride=sweeps), :] = y
        return carry

    lax.fori_loop(0, sweeps // batch, transform, 0)

    def gather(band, carry):
        for m in range(members):
            for p in range(2):
                row = (p * coarse + m * bands + band) * sweeps
                out_ref[m, p, band] = ys[pl.ds(pl.multiple_of(row, 16), sweeps), :].astype(BF16)
        return carry

    lax.fori_loop(0, bands, gather, 0, unroll=2)


def range_transform(x, members):
    _, sweeps, frequencies = x.shape
    coarse = frequencies // SIDE
    w1, w2, turning = transform_tables(frequencies)
    return pl.pallas_call(
        transform_kernel,
        out_shape=jax.ShapeDtypeStruct((members, 2, coarse // members, sweeps, SIDE), BF16),
        in_specs=[pl.BlockSpec(memory_space=pltpu.VMEM)] * 4,
        out_specs=pl.BlockSpec(memory_space=pltpu.VMEM),
        scratch_shapes=[
            pltpu.VMEM((2 * coarse * sweeps, SIDE), F32),
            pltpu.VMEM((2 * coarse * sweeps, SIDE), F32),
        ],
        compiler_params=pltpu.CompilerParams(vmem_limit_bytes=VMEM_LIMIT),
    )(x, jnp.asarray(w1), jnp.asarray(w2), jnp.asarray(turning))


def image_kernel(
    owners_ref, spec_ref, angle_ref, tilt_ref, slant_ref, lead_ref, weight_ref, out_ref,
    lhs, stencils, acc, tilt_tab, slant_tab,
):
    members, _, bands, sweeps, _ = spec_ref.shape
    angles, all_sweeps = angle_ref.shape
    groups = out_ref.shape[0]
    tilts = angles // SIDE
    factor = 1.0 / math.sqrt(all_sweeps)

    for a in range(0, angles, SIDE):
        rows = slice(a, a + SIDE)
        c, s = cos_sin(angle_ref[rows, :])
        c, s = c * factor, s * factor
        lhs[rows, :all_sweeps] = c.astype(BF16)
        lhs[rows, all_sweeps:] = (-s).astype(BF16)
        low = slice(angles + a, angles + a + SIDE)
        lhs[low, :all_sweeps] = s.astype(BF16)
        lhs[low, all_sweeps:] = c.astype(BF16)

    along = lax.broadcasted_iota(jnp.int32, (SIDE, SIDE), 0).astype(F32)
    c, s = cos_sin(along * tilt_ref[...])
    tilt_tab[0] = c
    tilt_tab[1] = s
    across = lax.broadcasted_iota(jnp.int32, (slant_ref.shape[0], SIDE), 1).astype(F32)
    c, s = cos_sin(across * slant_ref[...])
    slant_tab[0] = c
    slant_tab[1] = s

    f = weight_ref[...]
    taps = [
        -f * (f - 1.0) * (f - 2.0) / 6.0,
        (f + 1.0) * (f - 1.0) * (f - 2.0) / 2.0,
        -(f + 1.0) * f * (f - 2.0) / 2.0,
        (f + 1.0) * f * (f - 1.0) / 6.0,
    ]
    lead = lead_ref[...]
    cells = lax.broadcasted_iota(jnp.int32, (SIDE, SIDE), 1)
    for g in range(groups):
        for d in range(2):
            column = slice(g * 2 + d, g * 2 + d + 1)
            distance = cells - lead[:, column]
            total = jnp.zeros((SIDE, SIDE), F32)
            for q in range(4):
                total = total + jnp.where(distance == q, taps[q][:, column], 0.0)
            stencils[g, d] = total.astype(BF16)

    acc[...] = jnp.zeros_like(acc)
    pair = 2

    def step(i, carry):
        rhs = []
        for p in range(2):
            for m in range(members):
                rhs.append(jnp.concatenate([spec_ref[m, p, i * pair + j] for j in range(pair)], axis=1))
        rhs = jnp.concatenate(rhs, axis=0)
        shift = lax.rem(SIDE - i * pair * tilts, SIDE)
        cu = pltpu.roll(tilt_tab[0], shift, 1)
        su = pltpu.roll(tilt_tab[1], shift, 1)
        for ab in range(tilts):
            rows = slice(ab * SIDE, (ab + 1) * SIDE)
            low = slice(angles + ab * SIDE, angles + (ab + 1) * SIDE)
            re_pair = jnp.dot(lhs[rows, :], rhs, preferred_element_type=F32)
            im_pair = jnp.dot(lhs[low, :], rhs, preferred_element_type=F32)
            for j in range(pair):
                b = ab * bands + i * pair + j
                re = re_pair[:, j * SIDE:(j + 1) * SIDE]
                im = im_pair[:, j * SIDE:(j + 1) * SIDE]
                lane = j * tilts + ab
                cb = cu[:, lane:lane + 1]
                sb = su[:, lane:lane + 1]
                cv = slant_tab[0, pl.ds(b, 1), :]
                sv = slant_tab[1, pl.ds(b, 1), :]
                cosine = cb * cv - sb * sv
                sine = sb * cv + cb * sv
                demod = jnp.concatenate(
                    [(re * cosine - im * sine).astype(BF16), (re * sine + im * cosine).astype(BF16)], axis=1
                )
                owner = owners_ref[b]
                rows_done = jnp.dot(stencils[owner, 0], demod, preferred_element_type=F32).astype(BF16)
                rows_done = jnp.concatenate([rows_done[:, :SIDE], rows_done[:, SIDE:]], axis=0)
                acc[owner] += lax.dot_general(
                    rows_done, stencils[owner, 1], (((1,), (1,)), ((), ())), preferred_element_type=F32
                )
        return carry

    lax.fori_loop(0, bands // pair, step, 0)
    out_ref[...] = acc[...].astype(BF16)


def form_tiles(owners, spec, angles, slopes, lead, weight, groups):
    bands = spec.shape[2]
    tilts = angles.shape[0] // SIDE
    blocks = tilts * bands
    tilt = slopes[0].reshape(tilts, bands).T.reshape(1, blocks)
    tilt = jnp.pad(tilt, ((0, 0), (0, SIDE - blocks)))
    vmem = pl.BlockSpec(memory_space=pltpu.VMEM)
    return pl.pallas_call(
        image_kernel,
        out_shape=jax.ShapeDtypeStruct((groups, 2 * SIDE, SIDE), BF16),
        in_specs=[pl.BlockSpec(memory_space=pltpu.SMEM)] + [vmem] * 6,
        out_specs=vmem,
        scratch_shapes=[
            pltpu.VMEM((2 * angles.shape[0], 2 * angles.shape[1]), BF16),
            pltpu.VMEM((groups, 2, SIDE, SIDE), BF16),
            pltpu.VMEM((groups, 2 * SIDE, SIDE), F32),
            pltpu.VMEM((2, SIDE, SIDE), F32),
            pltpu.VMEM((2, blocks, SIDE), F32),
        ],
        compiler_params=pltpu.CompilerParams(vmem_limit_bytes=VMEM_LIMIT),
    )(owners, spec, angles, tilt, slopes[1][:, None], lead, weight)


def on_device(echo, angles, holder, slopes, lead, weight, *, groups, members):
    packed = jnp.concatenate([lead[0, 0].astype(F32), weight[0, 0]], axis=0)
    gathered = lax.all_gather(packed[None], "sub", axis=0, tiled=True)
    columns = jnp.transpose(gathered, (2, 0, 1))
    all_lead = columns[:, :, :2].reshape(SIDE, 2 * groups).astype(jnp.int32)
    all_weight = columns[:, :, 2:].reshape(SIDE, 2 * groups)
    spec = range_transform(echo[0], members)
    spec = lax.all_to_all(spec, "mem", split_axis=0, concat_axis=0, tiled=True)
    tiles = form_tiles(holder[0, 0], spec, angles[0, 0], slopes[0, 0], all_lead, all_weight, groups)
    parts = lax.all_to_all(tiles, "sub", split_axis=0, concat_axis=0, tiled=True)
    total = 0.25 * jnp.sum(parts.astype(F32), axis=0)
    return total.astype(BF16).reshape(1, 2, SIDE, SIDE)


def solution(mesh):
    return jax.shard_map(
        functools.partial(on_device, groups=mesh.shape["sub"], members=mesh.shape["mem"]),
        mesh=mesh,
        in_specs=(
            P("sub", None, "mem", None),
            P("sub", "mem", None, None),
            P("sub", "mem", None),
            P("sub", "mem", None, None),
            P("sub", "mem", None, None),
            P("sub", "mem", None, None),
        ),
        out_specs=P(("sub", "mem"), None, None, None),
        check_vma=False,
    )
```

time: 181 us -> 85.1 us (0.47)
  other arithmetic: 39.3 us -> 0.73 us
  local copies, waits for them, and re-layouts: 41.1 us -> 6.03 us
  matrix products: 32.6 us -> 0 us
  Pallas kernels: 0 us -> 28.1 us
  waiting for transfers between devices: 33.1 us -> 11.3 us
  blocking collectives: 15.3 us -> 33.1 us
  between operations: 13.5 us -> 0.08 us
    dot_general x6 -> x0, matrix products: 32.6 us -> none  [the longest x1 11.9 us: on_device(): jnp.einsum('ACo,ACpyx->opyx', picker.astype(jnp.float32), interpolated, p...]
    reduce_scatter x1 -> x0, waiting for transfers between devices: 31.5 us -> none  [on_device(): lax.psum_scatter(contributions.astype(jnp.bfloat16), 'sub', scatter_dimen...]
    pallas_call x0 -> x2, Pallas kernels: none -> 28.1 us  [the longest x1 17 us: form_tiles(): pl.pallas_call(image_kernel, out_shape=jax.ShapeDtypeStruct((groups, 2 *...]
    another operation x4 -> x0, other arithmetic: 20.8 us -> none
    all_to_all x0 -> x1, blocking collectives: none -> 20.2 us  [on_device(): lax.all_to_all(tiles, 'sub', split_axis=0, concat_axis=0, tiled=True)]
    add x4 -> x0, local copies, waits for them, and re-layouts: 17 us -> none  [combine(): return (product[0, 0] - product[1, 1], product[0, 1] + product[1, 0])]
    sub x4 -> x0, local copies, waits for them, and re-layouts: 16 us -> none  [combine(): return (product[0, 0] - product[1, 1], product[0, 1] + product[1, 0])]
    sub x2 -> x0, other arithmetic: 13.4 us -> none  [combine(): return (product[0, 0] - product[1, 1], product[0, 1] + product[1, 0])]
  transfers between devices with their start and end apart: 2 -> 1, of which waited for: 2 -> 1; matrix products, arithmetic and copies ran while one was open for 4% -> 1% of each run, Pallas kernels for 0% -> 0%
where the time goes in v1:
time: 85.1 us; the launch traced here: 84.7 us
  blocking collectives  33.1 us (39%)
  Pallas kernels  28.1 us (33%)
  waiting for transfers between devices  11.3 us (13%)
  local copies, waits for them, and re-layouts  6.03 us (7%)
  starting transfers between devices  5.31 us (6%)
    all_to_all x1, blocking collectives, on_device(): lax.all_to_all(tiles, 'sub', split_axis=0, concat_axis=0, tiled=True)  20.2 us
    pallas_call x1, Pallas kernels, form_tiles(): pl.pallas_call(image_kernel, out_shape=jax.ShapeDtypeStruct((groups, 2 *...  17 us
    all_gather x1, blocking collectives, on_device(): gathered = lax.all_gather(packed[None], 'sub', axis=0, tiled=True)  12.9 us
    all_to_all x1, waiting for transfers between devices, on_device(): spec = lax.all_to_all(spec, 'mem', split_axis=0, concat_axis=0, tiled=True)  11.3 us
    pallas_call x1, Pallas kernels, range_transform(): pl.pallas_call(transform_kernel, out_shape=jax.ShapeDtypeStruct((members,...  11.1 us
    unnamed x20, local copies, waits for them, and re-layouts  5.45 us
    all_to_all x1, starting transfers between devices, on_device(): spec = lax.all_to_all(spec, 'mem', split_axis=0, concat_axis=0, tiled=True)  5.31 us
  transfers between devices with their start and end apart: 1, of which 1 were waited for; matrix products, arithmetic and copies ran while one was open for 1% of the time, Pallas kernels for 0%

profile of v1, /device:TPU:0, one launch (start us, length us, event | category | flops | bytes accessed | tf_op | source)
XLA Modules:
  0.0 84.7 jit_solution(2650017259506324094)
XLA Ops:
  0.0 0.0 copy-start.1
  0.0 1.6 %copy-done.1 = bf16[1,2,64,8192]{3,2,1,0:T(8,128)(2,1)S(1)} copy-done((bf16[1,2,64,8192]{3,2,1,0:T(8,128)(2,1)S(1)}, bf16[1,2,64,8192]{3,2,1,0:T(8,128)(2,1)}, u32[]{:S(2)}) %copy-start.1) | copy-done | bytes 2097176
  1.6 0.0 copy-start.3
  1.6 0.9 %copy-done.3 = f32[2,128,128]{2,1,0:T(8,128)S(1)} copy-done((f32[2,128,128]{2,1,0:T(8,128)S(1)}, f32[2,128,128]{2,1,0:T(8,128)}, u32[]{:S(2)}) %copy-start.3) | copy-done | bytes 131096
  2.5 0.0 copy-start.4
  2.5 0.8 copy-done.4
  3.3 0.0 copy-start.5
  3.3 0.8 copy-done.5
  4.1 11.1 %shard_map.91 = bf16[4,2,16,64,128]{4,3,2,1,0:T(8,128)(2,1)S(1)} custom-call(bf16[2,64,8192]{2,1,0:T(8,128)(2,1)S(1)} %bitcast.15, bf16[128,128]{1,0:T(8,128)(2,1)S(1)} %copy-done.5, bf16[128,256]{1,0:T(8,128)(2,1)S(1)} %copy-done.4, f32[2,128,128]{2,1,0:T(8,128)S(1)} %copy-done.3), custom_call_target="tpu_custom_call" | custom-call | tf_op jit(solution)/shard_map/pallas_call | solution.py:103
  15.2 0.0 copy-start
  15.3 1.3 %copy-done = bf16[4,2,16,64,128]{4,3,2,1,0:T(8,128)(2,1)} copy-done((bf16[4,2,16,64,128]{4,3,2,1,0:T(8,128)(2,1)}, bf16[4,2,16,64,128]{4,3,2,1,0:T(8,128)(2,1)S(1)}, u32[]{:S(2)}) %copy-start) | copy-done | bytes 2097176
  16.6 0.0 copy-start.7
  16.6 0.0 copy-start.8
  16.6 0.0 copy-start.9
  16.6 0.0 copy-start.2
  16.6 0.0 copy-start.6
  16.6 5.3 %all-to-all-start = ((bf16[4,2,16,64,128]{4,3,2,1,0:T(8,128)(2,1)}), bf16[4,2,16,64,128]{4,3,2,1,0:T(8,128)(2,1)S(1)}, u32[]{:S(2)}, u32[]{:S(2)}) async-start(bf16[4,2,16,64,128]{4,3,2,1,0:T(8,128)(2,1)} %copy-done), calls=%async_computation | async-start | bytes 4194304 | tf_op jit(solution)/shard_map/all_to_all | solution.py:236
  21.9 0.0 copy-done.7
  21.9 0.1 reshape_squeeze.3
  22.0 0.1 copy.18
  22.1 0.1 reshape.30
  22.2 0.1 copy.19.slant_ref
  22.3 0.0 copy-done.8
  22.3 0.0 copy-done.9
  22.3 12.9 %all-gather.1 = f32[8,4,128]{2,1,0:T(4,128)S(1)} all-gather(f32[1,4,128]{2,1,0:T(4,128)S(1)} %maximum_bitcast_fusion), channel_id=2, replica_groups=mesh['sub'=8,'mem'=4] {'sub'}, dimensions={0}, use_global_device_ids=true | all-gather | bytes 18432 | tf_op jit(solution)/shard_map/all_gather | solution.py:231
  35.3 0.1 copy.20.lead_ref
  35.4 0.1 copy.21.weight_ref
  35.5 11.3 %all-to-all-done.spec_ref = bf16[4,2,16,64,128]{4,3,2,1,0:T(8,128)(2,1)S(1)} async-done(((bf16[4,2,16,64,128]{4,3,2,1,0:T(8,128)(2,1)}), bf16[4,2,16,64,128]{4,3,2,1,0:T(8,128)(2,1)S(1)}, u32[]{:S(2)}, u32[]{:S(2)}) %all-to-all-start) | async-done | bytes 2097184 | tf_op jit(solution)/shard_map/all_to_all | solution.py:236
  46.8 0.0 copy-done.2
  46.8 0.0 copy-done.6
  46.8 17.0 %shard_map.92 = bf16[8,256,128]{2,1,0:T(8,128)(2,1)S(1)} custom-call(s32[64]{0:T(128)S(1)} %bitcast.17, bf16[4,2,16,64,128]{4,3,2,1,0:T(8,128)(2,1)S(1)} %all-to-all-done.spec_ref, f32[512,256]{1,0:T(8,128)S(1)} %bitcast.16, f32[1,128]{1,0:T(1,128)S(1)} %pad.4.tilt_ref, f32[64,1]{1,0:T(8,128)S(1)} %copy.19.slant_ref, s32[128,16]{1,0:T(8,128)S(1)} %copy.20.lead_ref, ...), custom_call_target="tpu_custom_call" | custom-call | tf_op jit(solution)/shard_map/pallas_call | solution.py:213
  63.8 20.2 %all_to_all.10 = bf16[8,256,128]{2,1,0:T(8,128)(2,1)S(1)} all-to-all(bf16[8,256,128]{2,1,0:T(8,128)(2,1)S(1)} %shard_map.92), channel_id=1, replica_groups=mesh['sub'=8,'mem'=4] {'sub'}, dimensions={0} | all-to-all | bytes 1048576 | tf_op jit(solution)/shard_map/all_to_all | solution.py:238
  84.0 0.1 convert_reduce_fusion
  84.1 0.6 multiply_convert_fusion
  (5 shorter events, 0.0 us)
Async XLA Ops:
  0.0 1.6 %copy-start.1 = (bf16[1,2,64,8192]{3,2,1,0:T(8,128)(2,1)S(1)}, bf16[1,2,64,8192]{3,2,1,0:T(8,128)(2,1)}, u32[]{:S(2)}) copy-start(bf16[1,2,64,8192]{3,2,1,0:T(8,128)(2,1)} %param.9) | copy-start | bytes 6291460
  1.6 0.9 %copy-start.3 = (f32[2,128,128]{2,1,0:T(8,128)S(1)}, f32[2,128,128]{2,1,0:T(8,128)}, u32[]{:S(2)}) copy-start(f32[2,128,128]{2,1,0:T(8,128)} %constant.14.clone.turn_ref) | copy-start | bytes 393220
  2.5 0.8 copy-start.4
  3.3 0.8 copy-start.5
  15.2 1.3 %copy-start = (bf16[4,2,16,64,128]{4,3,2,1,0:T(8,128)(2,1)}, bf16[4,2,16,64,128]{4,3,2,1,0:T(8,128)(2,1)S(1)}, u32[]{:S(2)}) copy-start(bf16[4,2,16,64,128]{4,3,2,1,0:T(8,128)(2,1)S(1)} %shard_map.91) | copy-start | bytes 6291460
  16.6 5.3 %copy-start.7 = (f32[1,1,2,64]{3,2,1,0:T(2,128)S(1)}, f32[1,1,2,64]{3,2,1,0:T(2,128)}, u32[]{:S(2)}) copy-start(f32[1,1,2,64]{3,2,1,0:T(2,128)} %param.12) | copy-start | bytes 1540
  16.6 5.7 %copy-start.8 = (s32[1,1,2,128]{3,2,1,0:T(2,128)S(1)}, s32[1,1,2,128]{3,2,1,0:T(2,128)}, u32[]{:S(2)}) copy-start(s32[1,1,2,128]{3,2,1,0:T(2,128)} %param.13) | copy-start | bytes 3076
  16.6 5.7 %copy-start.9 = (f32[1,1,2,128]{3,2,1,0:T(2,128)S(1)}, f32[1,1,2,128]{3,2,1,0:T(2,128)}, u32[]{:S(2)}) copy-start(f32[1,1,2,128]{3,2,1,0:T(2,128)} %param.14) | copy-start | bytes 3076
  16.6 30.2 %copy-start.2 = (f32[1,1,512,256]{3,2,1,0:T(8,128)S(1)}, f32[1,1,512,256]{3,2,1,0:T(8,128)}, u32[]{:S(2)}) copy-start(f32[1,1,512,256]{3,2,1,0:T(8,128)} %param.10) | copy-start | bytes 1572868
  16.6 30.2 %copy-start.6 = (s32[1,1,64]{2,1,0:T(1,128)S(1)}, s32[1,1,64]{2,1,0:T(1,128)}, u32[]{:S(2)}) copy-start(s32[1,1,64]{2,1,0:T(1,128)} %param.11) | copy-start | bytes 772
  16.6 30.2 %all-to-all-start = ((bf16[4,2,16,64,128]{4,3,2,1,0:T(8,128)(2,1)}), bf16[4,2,16,64,128]{4,3,2,1,0:T(8,128)(2,1)S(1)}, u32[]{:S(2)}, u32[]{:S(2)}) async-start(bf16[4,2,16,64,128]{4,3,2,1,0:T(8,128)(2,1)} %copy-done), calls=%async_computation | async-start | bytes 4194304 | tf_op jit(solution)/shard_map/all_to_all | solution.py:236

commit v2 on v0

v2 whole, which is shorter than its diff:
```python
import functools
import math

import jax
import jax.numpy as jnp
from jax import lax
from jax.experimental import pallas as pl
from jax.experimental.pallas import tpu as pltpu
from jax.sharding import PartitionSpec as P

SIDE = 128
CHUNK = 16
PIECES = 2
F32 = jnp.float32
BF16 = jnp.bfloat16
I32 = jnp.int32
MESH = pl.DeviceIdType.MESH
VMEM_LIMIT = 56 * 1024 * 1024


def cos_sin(x):
    q = jnp.floor(x * (2.0 / math.pi) + 0.5)
    r = x - q * 1.5703125
    r = r - q * 4.837512969970703e-4
    r = r - q * 7.549789948768648e-8
    z = r * r
    s = r + r * z * (-1.6666654611e-1 + z * (8.3321608736e-3 + z * -1.9515295891e-4))
    c = 1.0 - 0.5 * z + z * z * (4.166664568298827e-2 + z * (-1.388731625493765e-3 + z * 2.443315711809948e-5))
    n = q.astype(jnp.int32)
    odd = (n & 1) == 1
    cos_base = jnp.where(odd, s, c)
    sin_base = jnp.where(odd, c, s)
    cos_neg = ((n + 1) & 2) == 2
    sin_neg = (n & 2) == 2
    return jnp.where(cos_neg, -cos_base, cos_base), jnp.where(sin_neg, -sin_base, sin_base)


def iota(rows, columns, dimension):
    return lax.broadcasted_iota(I32, (rows, columns), dimension)


def stacked_transform(coarse, columns):
    turns = (iota(coarse, columns, 0) * iota(coarse, columns, 1)) & (coarse - 1)
    c, s = cos_sin(turns.astype(F32) * (2.0 * math.pi / coarse))
    top = jnp.concatenate([c, -s], axis=1)
    low = jnp.concatenate([s, c], axis=1)
    return jnp.concatenate([top, low], axis=0).astype(BF16)


def down(row):
    return jnp.transpose(jnp.broadcast_to(row, (SIDE, SIDE)))


def stencil(lead_row, weight_row):
    f = down(weight_row)
    taps = [
        -f * (f - 1.0) * (f - 2.0) / 6.0,
        (f + 1.0) * (f - 1.0) * (f - 2.0) / 2.0,
        -(f + 1.0) * f * (f - 2.0) / 2.0,
        (f + 1.0) * f * (f - 1.0) / 6.0,
    ]
    distance = iota(SIDE, SIDE, 1).astype(F32) - down(lead_row.astype(F32))
    total = jnp.zeros((SIDE, SIDE), F32)
    for q in range(4):
        total = total + jnp.where(distance == q, taps[q], 0.0)
    return total.astype(BF16)


def kernel(
    groups, members,
    chain_ref, x_hbm, angle_hbm, slope_ref, lead_ref, weight_ref, out_ref,
    x, angle, xs, ys, w1s, w2s, turn, send, recv, lhs, polar, sums, tilt_tab, slant_tab, stencils,
    pair_out, pair_in, far_out, far_in, own,
    x_sem, angle_sem, mem_send, mem_recv, pair_send, pair_recv, far_send, far_recv,
):
    layers = groups // 2
    _, sweeps, frequencies = x.shape
    coarse = frequencies // SIDE
    bands = coarse // members
    half = bands // PIECES
    chunks = sweeps // CHUNK
    angles, all_sweeps = angle.shape
    tilts = angles // SIDE
    depth = 2 * members * CHUNK
    sub = lax.axis_index("sub")
    me = lax.axis_index("mem")
    layer, core = sub // 2, sub % 2
    partner = layer * 2 + 1 - core

    barrier = pltpu.get_barrier_semaphore()
    for d in range(1, members):
        pl.semaphore_signal(barrier, inc=1, device_id=(sub, (me + d) % members), device_id_type=MESH)
    pl.semaphore_signal(barrier, inc=1, device_id=(partner, me), device_id_type=MESH)
    for d in range(1, layers):
        other = ((layer + d) % layers) * 2 + core
        pl.semaphore_signal(barrier, inc=1, device_id=(other, me), device_id_type=MESH)

    def x_copy(q):
        rows = pl.ds(pl.multiple_of(q * CHUNK, CHUNK), CHUNK)
        return pltpu.make_async_copy(x_hbm.at[:, rows, :], x.at[:, rows, :], x_sem.at[q])

    for q in range(chunks):
        x_copy(q).start()
    angle_copy = pltpu.make_async_copy(angle_hbm, angle, angle_sem)
    angle_copy.start()

    w1s[...] = stacked_transform(coarse, coarse)
    w2s[...] = stacked_transform(coarse, SIDE)
    c, s = cos_sin((iota(SIDE, SIDE, 0) * iota(SIDE, SIDE, 1)).astype(F32) * (2.0 * math.pi / frequencies))
    turn[0] = c * (1.0 / math.sqrt(frequencies))
    turn[1] = s * (1.0 / math.sqrt(frequencies))

    pl.semaphore_wait(barrier, (members - 1) + 1 + (layers - 1))

    def mem_copy(q, piece, d):
        to = (me + d) % members
        return pltpu.make_async_remote_copy(
            src_ref=send.at[to, q, piece],
            dst_ref=recv.at[me, q, piece],
            send_sem=mem_send.at[d - 1, q, piece],
            recv_sem=mem_recv.at[d - 1, q, piece],
            device_id=(sub, to),
            device_id_type=MESH,
        )

    def transform(q, carry):
        x_copy(q).wait()
        rows = pl.ds(pl.multiple_of(q * CHUNK, CHUNK), CHUNK)

        def spread(k2, inner):
            lanes = pl.ds(pl.multiple_of(k2 * SIDE, SIDE), SIDE)
            for p in range(2):
                at = pl.ds(pl.multiple_of((p * coarse + k2) * CHUNK, CHUNK), CHUNK)
                xs[at, :] = x[p, rows, lanes].astype(F32)
            return inner

        lax.fori_loop(0, coarse, spread, 0, unroll=8)

        batch = 8

        def sweep_batch(step, inner):
            w1 = w1s[...]
            w2 = w2s[...]
            for j in range(batch):
                at = pl.ds(step * batch + j, 2 * coarse, stride=CHUNK)
                f = jnp.dot(w1, xs[at, :].astype(BF16), preferred_element_type=F32)
                re = jnp.concatenate([f[:coarse], f[:coarse]], axis=0)
                im = jnp.concatenate([f[coarse:], f[coarse:]], axis=0)
                cosine, sine = turn[0], turn[1]
                turned = jnp.concatenate(
                    [(re * cosine - im * sine).astype(BF16), (re * sine + im * cosine).astype(BF16)], axis=1
                )
                ys[at, :] = lax.dot_general(w2, turned, (((1,), (1,)), ((), ())), preferred_element_type=F32)
            return inner

        lax.fori_loop(0, CHUNK // batch, sweep_batch, 0)

        def pack(m, inner):
            for piece in range(PIECES):
                for p in range(2):
                    for band in range(half):
                        row = (p * coarse + m * bands + piece * half + band) * CHUNK
                        send[m, q, piece, p, band] = ys[pl.ds(pl.multiple_of(row, CHUNK), CHUNK), :].astype(BF16)
            return inner

        lax.fori_loop(0, members, pack, 0)
        for piece in range(PIECES):
            for d in range(1, members):
                mem_copy(q, piece, d).start()
        return carry

    lax.fori_loop(0, chunks, transform, 0)

    angle_copy.wait()
    factor = 1.0 / math.sqrt(all_sweeps)
    wide = 2 * all_sweeps
    source = iota(wide, wide, 0)
    k = iota(wide, wide, 1)
    q_of, p_of = k // depth, (k // (depth // 2)) % 2
    position = ((k // CHUNK) % members) * sweeps + q_of * CHUNK + k % CHUNK
    cos_at = (source == position).astype(F32)
    sin_at = (source == position + all_sweeps).astype(F32)
    first = p_of == 0
    place_re = jnp.where(first, cos_at, -sin_at).astype(BF16)
    place_im = jnp.where(first, sin_at, cos_at).astype(BF16)
    for a in range(tilts):
        c, s = cos_sin(angle[a * SIDE:(a + 1) * SIDE, :])
        table = jnp.concatenate([(c * factor).astype(BF16), (s * factor).astype(BF16)], axis=1)
        lhs[a, 0] = jnp.dot(table, place_re, preferred_element_type=F32).astype(BF16)
        lhs[a, 1] = jnp.dot(table, place_im, preferred_element_type=F32).astype(BF16)

    blocks = slope_ref.shape[1]
    tilt_tab[...] = jnp.zeros_like(tilt_tab)
    tilt_tab[0, :2, :blocks] = slope_ref[...]
    slopes = tilt_tab[0, :2, :]
    tilt_angles = iota(SIDE, SIDE, 0).astype(F32) * slopes[0:1, :]
    slant_angles = iota(SIDE, SIDE, 1).astype(F32) * down(slopes[1:2, :])
    c, s = cos_sin(tilt_angles)
    tilt_tab[0] = c
    tilt_tab[1] = s
    c, s = cos_sin(slant_angles)
    slant_tab[0] = c
    slant_tab[1] = s
    for d in range(2):
        stencils[d] = stencil(lead_ref[d:d + 1, :], weight_ref[d:d + 1, :])
    sums[0] = jnp.zeros((2 * SIDE, SIDE), F32)

    def keep_own(q, carry):
        recv[me, q] = send[me, q]
        return carry

    lax.fori_loop(0, chunks, keep_own, 0)

    def columns(piece, i, q):
        return jnp.concatenate(
            [
                jnp.concatenate([recv[m, q, piece, p, i * 2 + j] for j in range(2)], axis=1)
                for p in range(2)
                for m in range(members)
            ],
            axis=0,
        )

    early = (chunks - 1) * depth
    if chunks > 1:
        def early_wait(q, carry):
            for piece in range(PIECES):
                for d in range(1, members):
                    mem_copy(q, piece, d).wait_recv()
            return carry

        lax.fori_loop(0, chunks - 1, early_wait, 0)
        for piece in range(PIECES):
            def early_step(i, carry, piece=piece):
                rhs = jnp.concatenate([columns(piece, i, q) for q in range(chunks - 1)], axis=0)
                for a in range(tilts):
                    for r in range(2):
                        polar[piece * (half // 2) + i, a, r] = jnp.dot(
                            lhs[a, r, :, :early], rhs, preferred_element_type=F32
                        )
                return carry

            lax.fori_loop(0, half // 2, early_step, 0)

    for piece in range(PIECES):
        for d in range(1, members):
            mem_copy(chunks - 1, piece, d).wait_recv()

        def late_step(i, carry, piece=piece):
            rhs = columns(piece, i, chunks - 1)
            band = piece * half + i * 2
            shift = (SIDE - band) % SIDE
            cu = pltpu.roll(tilt_tab[0], shift, 1)
            su = pltpu.roll(tilt_tab[1], shift, 1)
            for a in range(tilts):
                parts = []
                for r in range(2):
                    part = jnp.dot(lhs[a, r, :, early:], rhs, preferred_element_type=F32)
                    if chunks > 1:
                        part = part + polar[piece * (half // 2) + i, a, r]
                    parts.append(part)
                for j in range(2):
                    b = a * bands + band + j
                    re = parts[0][:, j * SIDE:(j + 1) * SIDE]
                    im = parts[1][:, j * SIDE:(j + 1) * SIDE]
                    lane = a * bands + j
                    cb = cu[:, lane:lane + 1]
                    sb = su[:, lane:lane + 1]
                    cv = slant_tab[0, pl.ds(b, 1), :]
                    sv = slant_tab[1, pl.ds(b, 1), :]
                    cosine = cb * cv - sb * sv
                    sine = sb * cv + cb * sv
                    demod = jnp.concatenate([re * cosine - im * sine, re * sine + im * cosine], axis=0)
                    place = (band // 2) * (2 * tilts) + a * 2 + j
                    sums[place + 1] = sums[chain_ref[b]] + demod
            return carry

        lax.fori_loop(0, half // 2, late_step, 0)

    def tile_sum(o):
        return sums[chain_ref[blocks + o]]

    def to_partner(z, carry):
        pair_out[z] = tile_sum(z * 2 + 1 - core).astype(BF16)
        return carry

    lax.fori_loop(0, layers, to_partner, 0)
    pair_copy = pltpu.make_async_remote_copy(
        src_ref=pair_out, dst_ref=pair_in, send_sem=pair_send, recv_sem=pair_recv,
        device_id=(partner, me), device_id_type=MESH,
    )
    pair_copy.start()
    pair_copy.wait_recv()

    def far_copy(d):
        to = (layer + d) % layers
        return pltpu.make_async_remote_copy(
            src_ref=far_out.at[d - 1], dst_ref=far_in.at[d - 1],
            send_sem=far_send.at[d - 1], recv_sem=far_recv.at[d - 1],
            device_id=(to * 2 + core, me), device_id_type=MESH,
        )

    for d in range(1, layers):
        z = (layer + d) % layers
        far_out[d - 1] = (tile_sum(z * 2 + core) + pair_in[z].astype(F32)).astype(BF16)
        far_copy(d).start()
    own[...] = tile_sum(layer * 2 + core) + pair_in[layer].astype(F32)
    for d in range(1, layers):
        far_copy(d).wait_recv()
        own[...] += far_in[d - 1].astype(F32)

    total = own[...].astype(BF16)
    total = jnp.concatenate([total[:SIDE], total[SIDE:]], axis=1)
    rows_done = jnp.dot(stencils[0], total, preferred_element_type=F32).astype(BF16)
    rows_done = jnp.concatenate([rows_done[:, :SIDE], rows_done[:, SIDE:]], axis=0)
    tile = lax.dot_general(rows_done, stencils[1], (((1,), (1,)), ((), ())), preferred_element_type=F32)
    out_ref[...] = (0.25 * tile).astype(BF16)

    def sent(q, carry):
        for piece in range(PIECES):
            for d in range(1, members):
                mem_copy(q, piece, d).wait_send()
        return carry

    lax.fori_loop(0, chunks, sent, 0)
    pair_copy.wait_send()
    for d in range(1, layers):
        far_copy(d).wait_send()


def block_chain(owners, groups, tilts):
    blocks = owners.shape[0]
    bands = blocks // tilts
    keys = jnp.concatenate([owners, jnp.arange(groups, dtype=I32)])

    def place(block):
        tilt, band = block // bands, block % bands
        return (band // 2) * (2 * tilts) + tilt * 2 + band % 2

    row = jnp.arange(blocks + groups, dtype=I32)[:, None]
    row = jnp.where(row < blocks, place(row), blocks)
    column = place(jnp.arange(blocks, dtype=I32)[None, :])
    follows = (keys[:, None] == owners[None, :]) & (column < row)
    return jnp.max(jnp.where(follows, column + 1, 0), axis=1)


def on_device(echo, angles, holder, slopes, lead, weight, *, groups, members):
    _, _, sweeps, frequencies = echo.shape
    _, _, angle_count, all_sweeps = angles.shape
    coarse = frequencies // SIDE
    half = coarse // members // PIECES
    chunks = sweeps // CHUNK
    tilts = angle_count // SIDE
    blocks = slopes.shape[3]
    layers = groups // 2
    exchange = (members, chunks, PIECES, 2, half, CHUNK, SIDE)
    vmem = pl.BlockSpec(memory_space=pltpu.VMEM)
    anywhere = pl.BlockSpec(memory_space=pl.ANY)
    dma = pltpu.SemaphoreType.DMA
    tile = pl.pallas_call(
        functools.partial(kernel, groups, members),
        out_shape=jax.ShapeDtypeStruct((2 * SIDE, SIDE), BF16),
        in_specs=[pl.BlockSpec(memory_space=pltpu.SMEM), anywhere, anywhere, vmem, vmem, vmem],
        out_specs=vmem,
        scratch_shapes=[
            pltpu.VMEM((2, sweeps, frequencies), BF16),
            pltpu.VMEM((angle_count, all_sweeps), F32),
            pltpu.VMEM((2 * coarse * CHUNK, SIDE), F32),
            pltpu.VMEM((2 * coarse * CHUNK, SIDE), F32),
            pltpu.VMEM((2 * coarse, 2 * coarse), BF16),
            pltpu.VMEM((2 * coarse, 2 * SIDE), BF16),
            pltpu.VMEM((2, SIDE, SIDE), F32),
            pltpu.VMEM(exchange, BF16),
            pltpu.VMEM(exchange, BF16),
            pltpu.VMEM((tilts, 2, SIDE, 2 * all_sweeps), BF16),
            pltpu.VMEM((PIECES * (half // 2), tilts, 2, SIDE, 2 * SIDE), F32),
            pltpu.VMEM((blocks + 1, 2 * SIDE, SIDE), F32),
            pltpu.VMEM((2, SIDE, SIDE), F32),
            pltpu.VMEM((2, SIDE, SIDE), F32),
            pltpu.VMEM((2, SIDE, SIDE), BF16),
            pltpu.VMEM((layers, 2 * SIDE, SIDE), BF16),
            pltpu.VMEM((layers, 2 * SIDE, SIDE), BF16),
            pltpu.VMEM((layers - 1, 2 * SIDE, SIDE), BF16),
            pltpu.VMEM((layers - 1, 2 * SIDE, SIDE), BF16),
            pltpu.VMEM((2 * SIDE, SIDE), F32),
            dma((chunks,)),
            dma,
            dma((members - 1, chunks, PIECES)),
            dma((members - 1, chunks, PIECES)),
            dma,
            dma,
            dma((layers - 1,)),
            dma((layers - 1,)),
        ],
        compiler_params=pltpu.CompilerParams(
            vmem_limit_bytes=VMEM_LIMIT, collective_id=0, has_side_effects=True
        ),
    )(block_chain(holder[0, 0], groups, tilts), echo[0], angles[0, 0], slopes[0, 0], lead[0, 0], weight[0, 0])
    return tile.reshape(1, 2, SIDE, SIDE)


def solution(mesh):
    return jax.shard_map(
        functools.partial(on_device, groups=mesh.shape["sub"], members=mesh.shape["mem"]),
        mesh=mesh,
        in_specs=(
            P("sub", None, "mem", None),
            P("sub", "mem", None, None),
            P("sub", "mem", None),
            P("sub", "mem", None, None),
            P("sub", "mem", None, None),
            P("sub", "mem", None, None),
        ),
        out_specs=P(("sub", "mem"), None, None, None),
        check_vma=False,
    )
```

time: 181 us -> 48.2 us (0.27)
  Pallas kernels: 0 us -> 43.8 us
  local copies, waits for them, and re-layouts: 41.1 us -> 1.48 us
  other arithmetic: 39.3 us -> 2.01 us
  waiting for transfers between devices: 33.1 us -> 0 us
  matrix products: 32.6 us -> 0 us
  blocking collectives: 15.3 us -> 0 us
  between operations: 13.5 us -> 0.01 us
  starting transfers between devices: 5.32 us -> 0 us
    pallas_call x0 -> x1, Pallas kernels: none -> 43.8 us  [on_device(): pl.pallas_call(functools.partial(kernel, groups, members), out_shape=jax....]
    dot_general x6 -> x0, matrix products: 32.6 us -> none  [the longest x1 11.9 us: on_device(): jnp.einsum('ACo,ACpyx->opyx', picker.astype(jnp.float32), interpolated, p...]
    reduce_scatter x1 -> x0, waiting for transfers between devices: 31.5 us -> none  [on_device(): lax.psum_scatter(contributions.astype(jnp.bfloat16), 'sub', scatter_dimen...]
    another operation x4 -> x0, other arithmetic: 20.8 us -> none
    add x4 -> x0, local copies, waits for them, and re-layouts: 17 us -> none  [combine(): return (product[0, 0] - product[1, 1], product[0, 1] + product[1, 0])]
    sub x4 -> x0, local copies, waits for them, and re-layouts: 16 us -> none  [combine(): return (product[0, 0] - product[1, 1], product[0, 1] + product[1, 0])]
    all_gather x1 -> x0, blocking collectives: 15.3 us -> none  [on_device(): all_tables = lax.all_gather(own_tables[None], 'sub', axis=0, tiled=True)]
    sub x2 -> x0, other arithmetic: 13.4 us -> none  [combine(): return (product[0, 0] - product[1, 1], product[0, 1] + product[1, 0])]
  transfers between devices with their start and end apart: 2 -> 0, of which waited for: 2 -> 0; matrix products, arithmetic and copies ran while one was open for 4% -> 0% of each run, Pallas kernels for 0% -> 0%
where the time goes in v2:
time: 48.2 us; the launch traced here: 47.3 us
  Pallas kernels  43.8 us (91%)
  other arithmetic  2.01 us (4%)
  local copies, waits for them, and re-layouts  1.48 us (3%)
    pallas_call x1, Pallas kernels, on_device(): pl.pallas_call(functools.partial(kernel, groups, members), out_shape=jax....  43.8 us
    unnamed x1, local copies, waits for them, and re-layouts  1.47 us
    reduce_max x1, other arithmetic, block_chain(): return jnp.max(jnp.where(follows, column + 1, 0), axis=1)  1.27 us

profile of v2, /device:TPU:0, one launch (start us, length us, event | category | flops | bytes accessed | tf_op | source)
XLA Modules:
  0.0 47.3 jit_solution(5998283142623759318)
XLA Ops:
  0.0 0.7 %compare_select_fusion = (s32[72]{0:T(128)S(1)}, s32[72]{0:T(128)S(1)}) fusion(s32[8]{0:T(128)S(1)} %iota.16, s32[64]{0:T(128)} %bitcast.10), kind=kLoop, calls=%fused_computation.5 | loop fusion | flops 2736 | bytes 864 | tf_op jit(solution)/shard_map/jit(_where)/select_n | solution.py:341
  0.7 1.3 %select_reduce_fusion.chain_ref = s32[72]{0:T(128)} fusion(s32[64]{0:T(128)S(1)} %get-tuple-element.8, s32[72]{0:T(128)S(1)} %get-tuple-element.5, s32[72]{0:T(128)S(1)} %get-tuple-element.6, s32[64]{0:T(128)S(1)} %get-tuple-element.7, s32[64]{0:T(128)} %bitcast.11), kind=kLoop, calls=%fused_computation | loop fusion | flops 22968 | bytes 1632 | tf_op jit(solution)/shard_map/reduce_max | solution.py:344
  2.0 43.8 %shard_map.64 = bf16[256,128]{1,0:T(8,128)(2,1)} custom-call(s32[72]{0:T(128)} %select_reduce_fusion.chain_ref, bf16[2,64,8192]{2,1,0:T(8,128)(2,1)} %bitcast.7, f32[512,256]{1,0:T(8,128)} %bitcast.8, f32[2,64]{1,0:T(2,128)} %bitcast.12, s32[2,128]{1,0:T(2,128)} %bitcast.13, f32[2,128]{1,0:T(2,128)} %bitcast.14), custom_call_target="tpu_custom_call" | custom-call | tf_op jit(solution)/shard_map/pallas_call | solution.py:360
  45.8 1.5 %copy.8 = bf16[1,2,128,128]{3,2,1,0:T(8,128)(2,1)} copy(bf16[1,2,128,128]{3,2,1,0:T(8,128)(2,1)} %bitcast.9) | data formatting | bytes 131072
  (2 shorter events, 0.0 us)

commit v3 on v2

--- a/solution.py
+++ b/solution.py
@@ -10,7 +10,6 @@
 
 SIDE = 128
 CHUNK = 16
-PIECES = 2
 F32 = jnp.float32
 BF16 = jnp.bfloat16
 I32 = jnp.int32
@@ -68,16 +67,17 @@
 
 def kernel(
     groups, members,
-    chain_ref, x_hbm, angle_hbm, slope_ref, lead_ref, weight_ref, out_ref,
-    x, angle, xs, ys, w1s, w2s, turn, send, recv, lhs, polar, sums, tilt_tab, slant_tab, stencils,
+    owner_ref, x_hbm, angle_hbm, slope_ref, lead_ref, weight_ref, out_ref,
+    x, angle, xs, ys, w1s, w2s, turn, send, recv, lhs, polar, sums, phase, row_tab, chain_rows, chain_ref, slant_tab, stencils,
     pair_out, pair_in, far_out, far_in, own,
-    x_sem, angle_sem, mem_send, mem_recv, pair_send, pair_recv, far_send, far_recv,
+    x_sem, angle_sem, chain_sem, mem_send, mem_recv, pair_send, pair_recv, far_send, far_recv,
 ):
     layers = groups // 2
     _, sweeps, frequencies = x.shape
     coarse = frequencies // SIDE
     bands = coarse // members
-    half = bands // PIECES
+    pieces = send.shape[2]
+    half = bands // pieces
     chunks = sweeps // CHUNK
     angles, all_sweeps = angle.shape
     tilts = angles // SIDE
@@ -110,22 +110,24 @@
     turn[0] = c * (1.0 / math.sqrt(frequencies))
     turn[1] = s * (1.0 / math.sqrt(frequencies))
 
-    pl.semaphore_wait(barrier, (members - 1) + 1 + (layers - 1))
-
-    def mem_copy(q, piece, d):
+    def mem_copies(q, d, only=None):
         to = (me + d) % members
-        return pltpu.make_async_remote_copy(
-            src_ref=send.at[to, q, piece],
-            dst_ref=recv.at[me, q, piece],
-            send_sem=mem_send.at[d - 1, q, piece],
-            recv_sem=mem_recv.at[d - 1, q, piece],
-            device_id=(sub, to),
-            device_id_type=MESH,
-        )
-
-    def transform(q, carry):
+        parts = [None] if q < chunks - 1 else range(pieces) if only is None else [only]
+        return [
+            pltpu.make_async_remote_copy(
+                src_ref=send.at[to, q] if piece is None else send.at[to, q, piece],
+                dst_ref=recv.at[me, q] if piece is None else recv.at[me, q, piece],
+                send_sem=mem_send.at[d - 1, q, piece or 0],
+                recv_sem=mem_recv.at[d - 1, q, piece or 0],
+                device_id=(sub, to),
+                device_id_type=MESH,
+            )
+            for piece in parts
+        ]
+
+    def transform(q):
         x_copy(q).wait()
-        rows = pl.ds(pl.multiple_of(q * CHUNK, CHUNK), CHUNK)
+        rows = slice(q * CHUNK, (q + 1) * CHUNK)
 
         def spread(k2, inner):
             lanes = pl.ds(pl.multiple_of(k2 * SIDE, SIDE), SIDE)
@@ -141,22 +143,30 @@
         def sweep_batch(step, inner):
             w1 = w1s[...]
             w2 = w2s[...]
-            for j in range(batch):
-                at = pl.ds(step * batch + j, 2 * coarse, stride=CHUNK)
-                f = jnp.dot(w1, xs[at, :].astype(BF16), preferred_element_type=F32)
-                re = jnp.concatenate([f[:coarse], f[:coarse]], axis=0)
-                im = jnp.concatenate([f[coarse:], f[coarse:]], axis=0)
-                cosine, sine = turn[0], turn[1]
-                turned = jnp.concatenate(
-                    [(re * cosine - im * sine).astype(BF16), (re * sine + im * cosine).astype(BF16)], axis=1
+            for j in range(0, batch, 2):
+                at = [pl.ds(step * batch + j + h, 2 * coarse, stride=CHUNK) for h in range(2)]
+                both = jnp.concatenate([xs[at[h], :].astype(BF16) for h in range(2)], axis=1)
+                f = jnp.dot(w1, both, preferred_element_type=F32)
+                turned = []
+                for h in range(2):
+                    part = f[:, h * SIDE:(h + 1) * SIDE]
+                    re = jnp.concatenate([part[:coarse], part[:coarse]], axis=0)
+                    im = jnp.concatenate([part[coarse:], part[coarse:]], axis=0)
+                    cosine, sine = turn[0], turn[1]
+                    turned.append(jnp.concatenate(
+                        [(re * cosine - im * sine).astype(BF16), (re * sine + im * cosine).astype(BF16)], axis=1
+                    ))
+                y = lax.dot_general(
+                    w2, jnp.concatenate(turned, axis=0), (((1,), (1,)), ((), ())), preferred_element_type=F32
                 )
-                ys[at, :] = lax.dot_general(w2, turned, (((1,), (1,)), ((), ())), preferred_element_type=F32)
+                for h in range(2):
+                    ys[at[h], :] = y[:, h * SIDE:(h + 1) * SIDE]
             return inner
 
         lax.fori_loop(0, CHUNK // batch, sweep_batch, 0)
 
         def pack(m, inner):
-            for piece in range(PIECES):
+            for piece in range(pieces):
                 for p in range(2):
                     for band in range(half):
                         row = (p * coarse + m * bands + piece * half + band) * CHUNK
@@ -164,12 +174,15 @@
             return inner
 
         lax.fori_loop(0, members, pack, 0)
-        for piece in range(PIECES):
-            for d in range(1, members):
-                mem_copy(q, piece, d).start()
-        return carry
-
-    lax.fori_loop(0, chunks, transform, 0)
+
+    for q in range(chunks):
+        transform(q)
+        if q == 0:
+            pl.semaphore_wait(barrier, (members - 1) + 1 + (layers - 1))
+        copies = [mem_copies(q, d) for d in range(1, members)]
+        for group in zip(*copies):
+            for copy in group:
+                copy.start()
 
     angle_copy.wait()
     factor = 1.0 / math.sqrt(all_sweeps)
@@ -190,17 +203,37 @@
         lhs[a, 1] = jnp.dot(table, place_im, preferred_element_type=F32).astype(BF16)
 
     blocks = slope_ref.shape[1]
-    tilt_tab[...] = jnp.zeros_like(tilt_tab)
-    tilt_tab[0, :2, :blocks] = slope_ref[...]
-    slopes = tilt_tab[0, :2, :]
-    tilt_angles = iota(SIDE, SIDE, 0).astype(F32) * slopes[0:1, :]
-    slant_angles = iota(SIDE, SIDE, 1).astype(F32) * down(slopes[1:2, :])
-    c, s = cos_sin(tilt_angles)
-    tilt_tab[0] = c
-    tilt_tab[1] = s
-    c, s = cos_sin(slant_angles)
+    row_tab[...] = jnp.zeros_like(row_tab)
+    row_tab[0:2, :blocks] = slope_ref[...]
+    row_tab[2:3, :blocks] = owner_ref[...].astype(F32)
+
+    def place(block):
+        tilt, band = block // bands, block % bands
+        return (band // 2) * (2 * tilts) + tilt * 2 + band % 2
+
+    owner_row = row_tab[2:3, :]
+    lane = iota(SIDE, SIDE, 1)
+    taken = iota(SIDE, SIDE, 0)
+    key = jnp.where(lane < blocks, jnp.broadcast_to(owner_row, (SIDE, SIDE)), (lane - blocks).astype(F32))
+    limit = jnp.where(lane < blocks, place(lane), blocks)
+    earlier = place(taken)
+    follows = (key == down(owner_row)) & (taken < blocks) & (earlier < limit)
+    chain = jnp.max(jnp.where(follows, earlier + 1, 0), axis=0, keepdims=True)
+    chain_rows[...] = jnp.broadcast_to(chain, chain_rows.shape)
+    chain_copy = pltpu.make_async_copy(chain_rows, chain_ref, chain_sem)
+    chain_copy.start()
+
+    c, s = cos_sin(iota(SIDE, SIDE, 1).astype(F32) * down(row_tab[1:2, :]))
     slant_tab[0] = c
     slant_tab[1] = s
+    tilt_cos, tilt_sin = cos_sin(iota(SIDE, SIDE, 0).astype(F32) * row_tab[0:1, :])
+    for b in range(blocks):
+        cb = tilt_cos[:, b:b + 1]
+        sb = tilt_sin[:, b:b + 1]
+        cv = slant_tab[0, b:b + 1, :]
+        sv = slant_tab[1, b:b + 1, :]
+        phase[b, 0] = cb * cv - sb * sv
+        phase[b, 1] = sb * cv + cb * sv
     for d in range(2):
         stencils[d] = stencil(lead_ref[d:d + 1, :], weight_ref[d:d + 1, :])
     sums[0] = jnp.zeros((2 * SIDE, SIDE), F32)
@@ -221,18 +254,16 @@
             axis=0,
         )
 
-    early = (chunks - 1) * depth
-    if chunks > 1:
-        def early_wait(q, carry):
-            for piece in range(PIECES):
-                for d in range(1, members):
-                    mem_copy(q, piece, d).wait_recv()
-            return carry
-
-        lax.fori_loop(0, chunks - 1, early_wait, 0)
-        for piece in range(PIECES):
+    held = max(chunks - 2, 0)
+    early = held * depth
+    if held:
+        for q in range(held):
+            for d in range(1, members):
+                for copy in mem_copies(q, d):
+                    copy.wait_recv()
+        for piece in range(pieces):
             def early_step(i, carry, piece=piece):
-                rhs = jnp.concatenate([columns(piece, i, q) for q in range(chunks - 1)], axis=0)
+                rhs = jnp.concatenate([columns(piece, i, q) for q in range(held)], axis=0)
                 for a in range(tilts):
                     for r in range(2):
                         polar[piece * (half // 2) + i, a, r] = jnp.dot(
@@ -242,43 +273,40 @@
 
             lax.fori_loop(0, half // 2, early_step, 0)
 
-    for piece in range(PIECES):
+    chain_copy.wait()
+    for q in range(held, chunks - 1):
         for d in range(1, members):
-            mem_copy(chunks - 1, piece, d).wait_recv()
+            for copy in mem_copies(q, d):
+                copy.wait_recv()
+    for piece in range(pieces):
+        for d in range(1, members):
+            mem_copies(chunks - 1, d, piece)[0].wait_recv()
 
         def late_step(i, carry, piece=piece):
-            rhs = columns(piece, i, chunks - 1)
+            rhs = jnp.concatenate([columns(piece, i, q) for q in range(held, chunks)], axis=0)
             band = piece * half + i * 2
-            shift = (SIDE - band) % SIDE
-            cu = pltpu.roll(tilt_tab[0], shift, 1)
-            su = pltpu.roll(tilt_tab[1], shift, 1)
             for a in range(tilts):
                 parts = []
                 for r in range(2):
                     part = jnp.dot(lhs[a, r, :, early:], rhs, preferred_element_type=F32)
-                    if chunks > 1:
+                    if held:
                         part = part + polar[piece * (half // 2) + i, a, r]
                     parts.append(part)
                 for j in range(2):
                     b = a * bands + band + j
                     re = parts[0][:, j * SIDE:(j + 1) * SIDE]
                     im = parts[1][:, j * SIDE:(j + 1) * SIDE]
-                    lane = a * bands + j
-                    cb = cu[:, lane:lane + 1]
-                    sb = su[:, lane:lane + 1]
-                    cv = slant_tab[0, pl.ds(b, 1), :]
-                    sv = slant_tab[1, pl.ds(b, 1), :]
-                    cosine = cb * cv - sb * sv
-                    sine = sb * cv + cb * sv
+                    cosine = phase[b, 0]
+                    sine = phase[b, 1]
                     demod = jnp.concatenate([re * cosine - im * sine, re * sine + im * cosine], axis=0)
-                    place = (band // 2) * (2 * tilts) + a * 2 + j
-                    sums[place + 1] = sums[chain_ref[b]] + demod
+                    at = (band // 2) * (2 * tilts) + a * 2 + j
+                    sums[at + 1] = sums[chain_ref[0, b]] + demod
             return carry
 
         lax.fori_loop(0, half // 2, late_step, 0)
 
     def tile_sum(o):
-        return sums[chain_ref[blocks + o]]
+        return sums[chain_ref[0, blocks + o]]
 
     def to_partner(z, carry):
         pair_out[z] = tile_sum(z * 2 + 1 - core).astype(BF16)
@@ -314,53 +342,36 @@
     rows_done = jnp.dot(stencils[0], total, preferred_element_type=F32).astype(BF16)
     rows_done = jnp.concatenate([rows_done[:, :SIDE], rows_done[:, SIDE:]], axis=0)
     tile = lax.dot_general(rows_done, stencils[1], (((1,), (1,)), ((), ())), preferred_element_type=F32)
-    out_ref[...] = (0.25 * tile).astype(BF16)
-
-    def sent(q, carry):
-        for piece in range(PIECES):
-            for d in range(1, members):
-                mem_copy(q, piece, d).wait_send()
-        return carry
-
-    lax.fori_loop(0, chunks, sent, 0)
+    out_ref[...] = tile
+
+    for q in range(chunks):
+        for d in range(1, members):
+            for copy in mem_copies(q, d):
+                copy.wait_send()
     pair_copy.wait_send()
     for d in range(1, layers):
         far_copy(d).wait_send()
-
-
-def block_chain(owners, groups, tilts):
-    blocks = owners.shape[0]
-    bands = blocks // tilts
-    keys = jnp.concatenate([owners, jnp.arange(groups, dtype=I32)])
-
-    def place(block):
-        tilt, band = block // bands, block % bands
-        return (band // 2) * (2 * tilts) + tilt * 2 + band % 2
-
-    row = jnp.arange(blocks + groups, dtype=I32)[:, None]
-    row = jnp.where(row < blocks, place(row), blocks)
-    column = place(jnp.arange(blocks, dtype=I32)[None, :])
-    follows = (keys[:, None] == owners[None, :]) & (column < row)
-    return jnp.max(jnp.where(follows, column + 1, 0), axis=1)
 
 
 def on_device(echo, angles, holder, slopes, lead, weight, *, groups, members):
     _, _, sweeps, frequencies = echo.shape
     _, _, angle_count, all_sweeps = angles.shape
     coarse = frequencies // SIDE
-    half = coarse // members // PIECES
+    bands = coarse // members
+    pieces = min(4, bands // 2)
+    half = bands // pieces
     chunks = sweeps // CHUNK
     tilts = angle_count // SIDE
     blocks = slopes.shape[3]
     layers = groups // 2
-    exchange = (members, chunks, PIECES, 2, half, CHUNK, SIDE)
+    exchange = (members, chunks, pieces, 2, half, CHUNK, SIDE)
     vmem = pl.BlockSpec(memory_space=pltpu.VMEM)
     anywhere = pl.BlockSpec(memory_space=pl.ANY)
     dma = pltpu.SemaphoreType.DMA
     tile = pl.pallas_call(
         functools.partial(kernel, groups, members),
-        out_shape=jax.ShapeDtypeStruct((2 * SIDE, SIDE), BF16),
-        in_specs=[pl.BlockSpec(memory_space=pltpu.SMEM), anywhere, anywhere, vmem, vmem, vmem],
+        out_shape=jax.ShapeDtypeStruct((2 * SIDE, SIDE), F32),
+        in_specs=[vmem, anywhere, anywhere, vmem, vmem, vmem],
         out_specs=vmem,
         scratch_shapes=[
             pltpu.VMEM((2, sweeps, frequencies), BF16),
@@ -373,9 +384,12 @@
             pltpu.VMEM(exchange, BF16),
             pltpu.VMEM(exchange, BF16),
             pltpu.VMEM((tilts, 2, SIDE, 2 * all_sweeps), BF16),
-            pltpu.VMEM((PIECES * (half // 2), tilts, 2, SIDE, 2 * SIDE), F32),
+            pltpu.VMEM((bands // 2, tilts, 2, SIDE, 2 * SIDE), F32),
             pltpu.VMEM((blocks + 1, 2 * SIDE, SIDE), F32),
-            pltpu.VMEM((2, SIDE, SIDE), F32),
+            pltpu.VMEM((blocks, 2, SIDE, SIDE), F32),
+            pltpu.VMEM((8, SIDE), F32),
+            pltpu.VMEM((8, SIDE), I32),
+            pltpu.SMEM((8, SIDE), I32),
             pltpu.VMEM((2, SIDE, SIDE), F32),
             pltpu.VMEM((2, SIDE, SIDE), BF16),
             pltpu.VMEM((layers, 2 * SIDE, SIDE), BF16),
@@ -385,8 +399,9 @@
             pltpu.VMEM((2 * SIDE, SIDE), F32),
             dma((chunks,)),
             dma,
-            dma((members - 1, chunks, PIECES)),
-            dma((members - 1, chunks, PIECES)),
+            dma,
+            dma((members - 1, chunks, pieces)),
+            dma((members - 1, chunks, pieces)),
             dma,
             dma,
             dma((layers - 1,)),
@@ -395,8 +410,8 @@
         compiler_params=pltpu.CompilerParams(
             vmem_limit_bytes=VMEM_LIMIT, collective_id=0, has_side_effects=True
         ),
-    )(block_chain(holder[0, 0], groups, tilts), echo[0], angles[0, 0], slopes[0, 0], lead[0, 0], weight[0, 0])
-    return tile.reshape(1, 2, SIDE, SIDE)
+    )(holder[0], echo[0], angles[0, 0], slopes[0, 0], lead[0, 0], weight[0, 0])
+    return (0.25 * tile).astype(BF16).reshape(1, 2, SIDE, SIDE)
 
 
 def solution(mesh):

time: 48.2 us -> 43.6 us (0.905)
  the two profiles are of different devices: /device:TPU:0 before, /device:TPU:1 now
where the time goes in v3:
time: 43.6 us; the launch traced here: 43.4 us
  Pallas kernels  41.8 us (96%)
  other arithmetic  1.54 us (4%)
    pallas_call x1, Pallas kernels, on_device(): pl.pallas_call(functools.partial(kernel, groups, members), out_shape=jax....  41.8 us
    convert_element_type x1, other arithmetic, on_device(): return (0.25 * tile).astype(BF16).reshape(1, 2, SIDE, SIDE)  1.54 us

profile of v3, /device:TPU:1, one launch (start us, length us, event | category | flops | bytes accessed | tf_op | source)
XLA Modules:
  0.0 43.4 jit_solution(15007497439672933424)
XLA Ops:
  0.0 41.8 %shard_map.64 = f32[256,128]{1,0:T(8,128)} custom-call(s32[1,64]{1,0:T(1,128)} %bitcast.12, bf16[2,64,8192]{2,1,0:T(8,128)(2,1)} %bitcast.7, f32[512,256]{1,0:T(8,128)} %bitcast.8, f32[2,64]{1,0:T(2,128)} %bitcast.9, s32[2,128]{1,0:T(2,128)} %bitcast.10, f32[2,128]{1,0:T(2,128)} %bitcast.11), custom_call_target="tpu_custom_call" | custom-call | tf_op jit(solution)/shard_map/pallas_call | solution.py:371
  41.8 1.5 %multiply_convert_fusion = bf16[256,128]{1,0:T(8,128)(2,1)} fusion(f32[256,128]{1,0:T(8,128)} %shard_map.64), kind=kLoop, calls=%fused_computation | loop fusion | flops 65536 | bytes 196608 | tf_op jit(solution)/shard_map/convert_element_type | solution.py:414

commit v4 on v3

--- a/solution.py
+++ b/solution.py
@@ -68,7 +68,7 @@
 def kernel(
     groups, members,
     owner_ref, x_hbm, angle_hbm, slope_ref, lead_ref, weight_ref, out_ref,
-    x, angle, xs, ys, w1s, w2s, turn, send, recv, lhs, polar, sums, phase, row_tab, chain_rows, chain_ref, slant_tab, stencils,
+    x, angle, xs, ys, w1s, w2s, turn, send, recv, lhs, polar, sums, phase, row_tab, chain_rows, chain_ref, tilt_tab, slant_tab, stencils,
     pair_out, pair_in, far_out, far_in, own,
     x_sem, angle_sem, chain_sem, mem_send, mem_recv, pair_send, pair_recv, far_send, far_recv,
 ):
@@ -110,24 +110,22 @@
     turn[0] = c * (1.0 / math.sqrt(frequencies))
     turn[1] = s * (1.0 / math.sqrt(frequencies))
 
-    def mem_copies(q, d, only=None):
+    def mem_copy(q, piece, d):
         to = (me + d) % members
-        parts = [None] if q < chunks - 1 else range(pieces) if only is None else [only]
-        return [
-            pltpu.make_async_remote_copy(
-                src_ref=send.at[to, q] if piece is None else send.at[to, q, piece],
-                dst_ref=recv.at[me, q] if piece is None else recv.at[me, q, piece],
-                send_sem=mem_send.at[d - 1, q, piece or 0],
-                recv_sem=mem_recv.at[d - 1, q, piece or 0],
-                device_id=(sub, to),
-                device_id_type=MESH,
-            )
-            for piece in parts
-        ]
-
-    def transform(q):
+        return pltpu.make_async_remote_copy(
+            src_ref=send.at[to, q, piece],
+            dst_ref=recv.at[me, q, piece],
+            send_sem=mem_send.at[d - 1, q, piece],
+            recv_sem=mem_recv.at[d - 1, q, piece],
+            device_id=(sub, to),
+            device_id_type=MESH,
+        )
+
+    pl.semaphore_wait(barrier, (members - 1) + 1 + (layers - 1))
+
+    def transform(q, carry):
         x_copy(q).wait()
-        rows = slice(q * CHUNK, (q + 1) * CHUNK)
+        rows = pl.ds(pl.multiple_of(q * CHUNK, CHUNK), CHUNK)
 
         def spread(k2, inner):
             lanes = pl.ds(pl.multiple_of(k2 * SIDE, SIDE), SIDE)
@@ -175,14 +173,12 @@
 
         lax.fori_loop(0, members, pack, 0)
 
-    for q in range(chunks):
-        transform(q)
-        if q == 0:
-            pl.semaphore_wait(barrier, (members - 1) + 1 + (layers - 1))
-        copies = [mem_copies(q, d) for d in range(1, members)]
-        for group in zip(*copies):
-            for copy in group:
-                copy.start()
+        for piece in range(pieces):
+            for d in range(1, members):
+                mem_copy(q, piece, d).start()
+        return carry
+
+    lax.fori_loop(0, chunks, transform, 0)
 
     angle_copy.wait()
     factor = 1.0 / math.sqrt(all_sweeps)
@@ -227,13 +223,24 @@
     slant_tab[0] = c
     slant_tab[1] = s
     tilt_cos, tilt_sin = cos_sin(iota(SIDE, SIDE, 0).astype(F32) * row_tab[0:1, :])
-    for b in range(blocks):
-        cb = tilt_cos[:, b:b + 1]
-        sb = tilt_sin[:, b:b + 1]
-        cv = slant_tab[0, b:b + 1, :]
-        sv = slant_tab[1, b:b + 1, :]
-        phase[b, 0] = cb * cv - sb * sv
-        phase[b, 1] = sb * cv + cb * sv
+    tilt_tab[0] = tilt_cos
+    tilt_tab[1] = tilt_sin
+
+    def make_phase(band, carry):
+        shift = (SIDE - band) % SIDE
+        cu = pltpu.roll(tilt_tab[0], shift, 1)
+        su = pltpu.roll(tilt_tab[1], shift, 1)
+        for a in range(tilts):
+            b = a * bands + band
+            cb = cu[:, a * bands:a * bands + 1]
+            sb = su[:, a * bands:a * bands + 1]
+            cv = slant_tab[0, pl.ds(b, 1), :]
+            sv = slant_tab[1, pl.ds(b, 1), :]
+            phase[b, 0] = cb * cv - sb * sv
+            phase[b, 1] = sb * cv + cb * sv
+        return carry
+
+    lax.fori_loop(0, bands, make_phase, 0)
     for d in range(2):
         stencils[d] = stencil(lead_ref[d:d + 1, :], weight_ref[d:d + 1, :])
     sums[0] = jnp.zeros((2 * SIDE, SIDE), F32)
@@ -256,69 +263,71 @@
 
     held = max(chunks - 2, 0)
     early = held * depth
+
+    def arrived(q, carry):
+        for piece in range(pieces):
+            for d in range(1, members):
+                mem_copy(q, piece, d).wait_recv()
+        return carry
+
+    pairs = half // 2
     if held:
-        for q in range(held):
-            for d in range(1, members):
-                for copy in mem_copies(q, d):
-                    copy.wait_recv()
-        for piece in range(pieces):
-            def early_step(i, carry, piece=piece):
-                rhs = jnp.concatenate([columns(piece, i, q) for q in range(held)], axis=0)
-                for a in range(tilts):
-                    for r in range(2):
-                        polar[piece * (half // 2) + i, a, r] = jnp.dot(
-                            lhs[a, r, :, :early], rhs, preferred_element_type=F32
-                        )
-                return carry
-
-            lax.fori_loop(0, half // 2, early_step, 0)
+        lax.fori_loop(0, held, arrived, 0)
+
+        def early_step(n, carry):
+            rhs = jnp.concatenate([columns(n // pairs, n % pairs, q) for q in range(held)], axis=0)
+            for a in range(tilts):
+                for r in range(2):
+                    polar[n, a, r] = jnp.dot(lhs[a, r, :, :early], rhs, preferred_element_type=F32)
+            return carry
+
+        lax.fori_loop(0, bands // 2, early_step, 0)
 
     chain_copy.wait()
-    for q in range(held, chunks - 1):
+    lax.fori_loop(held, chunks - 1, arrived, 0)
+
+    def late_piece(piece, carry):
         for d in range(1, members):
-            for copy in mem_copies(q, d):
-                copy.wait_recv()
-    for piece in range(pieces):
-        for d in range(1, members):
-            mem_copies(chunks - 1, d, piece)[0].wait_recv()
-
-        def late_step(i, carry, piece=piece):
+            mem_copy(chunks - 1, piece, d).wait_recv()
+
+        def late_step(i, inner):
+            n = piece * pairs + i
             rhs = jnp.concatenate([columns(piece, i, q) for q in range(held, chunks)], axis=0)
-            band = piece * half + i * 2
             for a in range(tilts):
                 parts = []
                 for r in range(2):
                     part = jnp.dot(lhs[a, r, :, early:], rhs, preferred_element_type=F32)
                     if held:
-                        part = part + polar[piece * (half // 2) + i, a, r]
+                        part = part + polar[n, a, r]
                     parts.append(part)
                 for j in range(2):
-                    b = a * bands + band + j
+                    b = a * bands + n * 2 + j
                     re = parts[0][:, j * SIDE:(j + 1) * SIDE]
                     im = parts[1][:, j * SIDE:(j + 1) * SIDE]
                     cosine = phase[b, 0]
                     sine = phase[b, 1]
                     demod = jnp.concatenate([re * cosine - im * sine, re * sine + im * cosine], axis=0)
-                    at = (band // 2) * (2 * tilts) + a * 2 + j
-                    sums[at + 1] = sums[chain_ref[0, b]] + demod
-            return carry
-
-        lax.fori_loop(0, half // 2, late_step, 0)
+                    sums[n * (2 * tilts) + a * 2 + j + 1] = sums[chain_ref[0, b]] + demod
+            return inner
+
+        lax.fori_loop(0, pairs, late_step, 0)
+        return carry
+
+    lax.fori_loop(0, pieces, late_piece, 0)
 
     def tile_sum(o):
         return sums[chain_ref[0, blocks + o]]
 
-    def to_partner(z, carry):
-        pair_out[z] = tile_sum(z * 2 + 1 - core).astype(BF16)
-        return carry
-
-    lax.fori_loop(0, layers, to_partner, 0)
-    pair_copy = pltpu.make_async_remote_copy(
-        src_ref=pair_out, dst_ref=pair_in, send_sem=pair_send, recv_sem=pair_recv,
-        device_id=(partner, me), device_id_type=MESH,
-    )
-    pair_copy.start()
-    pair_copy.wait_recv()
+    def pair_copy(d):
+        return pltpu.make_async_remote_copy(
+            src_ref=pair_out.at[d], dst_ref=pair_in.at[d], send_sem=pair_send.at[d], recv_sem=pair_recv.at[d],
+            device_id=(partner, me), device_id_type=MESH,
+        )
+
+    order = list(range(1, layers)) + [0]
+    for d in order:
+        pair_out[d] = tile_sum(((layer + d) % layers) * 2 + 1 - core).astype(BF16)
+        pair_copy(d).start()
 
     def far_copy(d):
         to = (layer + d) % layers
@@ -329,10 +338,12 @@
         )
 
     for d in range(1, layers):
-        z = (layer + d) % layers
-        far_out[d - 1] = (tile_sum(z * 2 + core) + pair_in[z].astype(F32)).astype(BF16)
+        mine = tile_sum(((layer + d) % layers) * 2 + core)
+        pair_copy(d).wait_recv()
+        far_out[d - 1] = (mine + pair_in[d].astype(F32)).astype(BF16)
         far_copy(d).start()
-    own[...] = tile_sum(layer * 2 + core) + pair_in[layer].astype(F32)
+    pair_copy(0).wait_recv()
+    own[...] = tile_sum(layer * 2 + core) + pair_in[0].astype(F32)
     for d in range(1, layers):
         far_copy(d).wait_recv()
         own[...] += far_in[d - 1].astype(F32)
@@ -344,11 +355,15 @@
     tile = lax.dot_general(rows_done, stencils[1], (((1,), (1,)), ((), ())), preferred_element_type=F32)
     out_ref[...] = tile
 
-    for q in range(chunks):
-        for d in range(1, members):
-            for copy in mem_copies(q, d):
-                copy.wait_send()
-    pair_copy.wait_send()
+    def sent(q, carry):
+        for piece in range(pieces):
+            for d in range(1, members):
+                mem_copy(q, piece, d).wait_send()
+        return carry
+
+    lax.fori_loop(0, chunks, sent, 0)
+    for d in order:
+        pair_copy(d).wait_send()
     for d in range(1, layers):
         far_copy(d).wait_send()
 
@@ -391,6 +406,7 @@
             pltpu.VMEM((8, SIDE), I32),
             pltpu.SMEM((8, SIDE), I32),
             pltpu.VMEM((2, SIDE, SIDE), F32),
+            pltpu.VMEM((2, SIDE, SIDE), F32),
             pltpu.VMEM((2, SIDE, SIDE), BF16),
             pltpu.VMEM((layers, 2 * SIDE, SIDE), BF16),
             pltpu.VMEM((layers, 2 * SIDE, SIDE), BF16),
@@ -402,8 +418,8 @@
             dma,
             dma((members - 1, chunks, pieces)),
             dma((members - 1, chunks, pieces)),
-            dma,
-            dma,
+            dma((layers,)),
+            dma((layers,)),
             dma((layers - 1,)),
             dma((layers - 1,)),
         ],

time: 43.6 us -> 43.7 us (level)
  the two profiles are of different devices: /device:TPU:1 before, /device:TPU:0 now
where the time goes in v4:
time: 43.7 us; the launch traced here: 43.1 us
  Pallas kernels  41.6 us (95%)
  other arithmetic  1.54 us (4%)
    pallas_call x1, Pallas kernels, on_device(): pl.pallas_call(functools.partial(kernel, groups, members), out_shape=jax....  41.6 us
    convert_element_type x1, other arithmetic, on_device(): return (0.25 * tile).astype(BF16).reshape(1, 2, SIDE, SIDE)  1.54 us

profile of v4, /device:TPU:0, one launch (start us, length us, event | category | flops | bytes accessed | tf_op | source)
XLA Modules:
  0.0 43.1 jit_solution(5369580897504366151)
XLA Ops:
  0.0 41.6 %shard_map.64 = f32[256,128]{1,0:T(8,128)} custom-call(s32[1,64]{1,0:T(1,128)} %bitcast.12, bf16[2,64,8192]{2,1,0:T(8,128)(2,1)} %bitcast.7, f32[512,256]{1,0:T(8,128)} %bitcast.8, f32[2,64]{1,0:T(2,128)} %bitcast.9, s32[2,128]{1,0:T(2,128)} %bitcast.10, f32[2,128]{1,0:T(2,128)} %bitcast.11), custom_call_target="tpu_custom_call" | custom-call | tf_op jit(solution)/shard_map/pallas_call | solution.py:386
  41.6 1.5 %multiply_convert_fusion = bf16[256,128]{1,0:T(8,128)(2,1)} fusion(f32[256,128]{1,0:T(8,128)} %shard_map.64), kind=kLoop, calls=%fused_computation | loop fusion | flops 65536 | bytes 196608 | tf_op jit(solution)/shard_map/convert_element_type | solution.py:430

commit v5 on v4

v5 whole, which is shorter than its diff:
```python
import functools
import math

import jax
import jax.numpy as jnp
from jax import lax
from jax.experimental import pallas as pl
from jax.experimental.pallas import tpu as pltpu
from jax.sharding import PartitionSpec as P

SIDE = 128
CHUNK = 16
F32 = jnp.float32
BF16 = jnp.bfloat16
I32 = jnp.int32
MESH = pl.DeviceIdType.MESH
VMEM_LIMIT = 56 * 1024 * 1024


def cos_sin(x):
    q = jnp.floor(x * (2.0 / math.pi) + 0.5)
    r = x - q * 1.5703125
    r = r - q * 4.837512969970703e-4
    r = r - q * 7.549789948768648e-8
    z = r * r
    s = r + r * z * (-1.6666654611e-1 + z * (8.3321608736e-3 + z * -1.9515295891e-4))
    c = 1.0 - 0.5 * z + z * z * (4.166664568298827e-2 + z * (-1.388731625493765e-3 + z * 2.443315711809948e-5))
    n = q.astype(jnp.int32)
    odd = (n & 1) == 1
    cos_base = jnp.where(odd, s, c)
    sin_base = jnp.where(odd, c, s)
    cos_neg = ((n + 1) & 2) == 2
    sin_neg = (n & 2) == 2
    return jnp.where(cos_neg, -cos_base, cos_base), jnp.where(sin_neg, -sin_base, sin_base)


def iota(rows, columns, dimension):
    return lax.broadcasted_iota(I32, (rows, columns), dimension)


def stacked_transform(coarse, columns):
    turns = (iota(coarse, columns, 0) * iota(coarse, columns, 1)) & (coarse - 1)
    c, s = cos_sin(turns.astype(F32) * (2.0 * math.pi / coarse))
    top = jnp.concatenate([c, -s], axis=1)
    low = jnp.concatenate([s, c], axis=1)
    return jnp.concatenate([top, low], axis=0).astype(BF16)


def down(row):
    return jnp.transpose(jnp.broadcast_to(row, (SIDE, SIDE)))


def stencil(lead_row, weight_row):
    f = down(weight_row)
    taps = [
        -f * (f - 1.0) * (f - 2.0) / 6.0,
        (f + 1.0) * (f - 1.0) * (f - 2.0) / 2.0,
        -(f + 1.0) * f * (f - 2.0) / 2.0,
        (f + 1.0) * f * (f - 1.0) / 6.0,
    ]
    distance = iota(SIDE, SIDE, 1).astype(F32) - down(lead_row.astype(F32))
    total = jnp.zeros((SIDE, SIDE), F32)
    for q in range(4):
        total = total + jnp.where(distance == q, taps[q], 0.0)
    return total.astype(BF16)


def kernel(
    groups, members,
    owner_ref, x_hbm, angle_hbm, slope_ref, lead_ref, weight_ref, out_ref,
    x, angle, xs, ys, w1s, w2s, turn, send0, recv0, send1, recv1, lhs, sums, row_tab, chain_rows, chain_ref, tilt_tab, slant_tab, stencils,
    pair_out, pair_in, far_out, far_in, own,
    x_sem, angle_sem, chain_sem, send_sem0, recv_sem0, send_sem1, recv_sem1, pair_send, pair_recv, far_send, far_recv,
):
    layers = groups // 2
    _, sweeps, frequencies = x.shape
    coarse = frequencies // SIDE
    bands = coarse // members
    pieces = send1.shape[1]
    half = bands // pieces
    chunks = sweeps // CHUNK
    angles, all_sweeps = angle.shape
    tilts = angles // SIDE
    sub = lax.axis_index("sub")
    me = lax.axis_index("mem")
    layer, core = sub // 2, sub % 2
    partner = layer * 2 + 1 - core

    barrier = pltpu.get_barrier_semaphore()
    for d in range(1, members):
        pl.semaphore_signal(barrier, inc=1, device_id=(sub, (me + d) % members), device_id_type=MESH)
    pl.semaphore_signal(barrier, inc=1, device_id=(partner, me), device_id_type=MESH)
    for d in range(1, layers):
        other = ((layer + d) % layers) * 2 + core
        pl.semaphore_signal(barrier, inc=1, device_id=(other, me), device_id_type=MESH)

    def x_copy(q):
        rows = pl.ds(pl.multiple_of(q * CHUNK, CHUNK), CHUNK)
        return pltpu.make_async_copy(x_hbm.at[:, rows, :], x.at[:, rows, :], x_sem.at[q])

    for q in range(chunks):
        x_copy(q).start()
    angle_copy = pltpu.make_async_copy(angle_hbm, angle, angle_sem)
    angle_copy.start()

    w1s[...] = stacked_transform(coarse, coarse)
    w2s[...] = stacked_transform(coarse, SIDE)
    c, s = cos_sin((iota(SIDE, SIDE, 0) * iota(SIDE, SIDE, 1)).astype(F32) * (2.0 * math.pi / frequencies))
    turn[0] = c * (1.0 / math.sqrt(frequencies))
    turn[1] = s * (1.0 / math.sqrt(frequencies))

    def mem_copy(h, n, d):
        to = (me + d) % members
        src, dst = ((send0, recv0), (send1, recv1))[h]
        send_sem, recv_sem = ((send_sem0, recv_sem0), (send_sem1, recv_sem1))[h]
        return pltpu.make_async_remote_copy(
            src_ref=src.at[to, n],
            dst_ref=dst.at[me, n],
            send_sem=send_sem.at[d - 1, n],
            recv_sem=recv_sem.at[d - 1, n],
            device_id=(sub, to),
            device_id_type=MESH,
        )

    pl.semaphore_wait(barrier, (members - 1) + 1 + (layers - 1))

    def transform(q, carry):
        x_copy(q).wait()
        rows = pl.ds(pl.multiple_of(q * CHUNK, CHUNK), CHUNK)

        def spread(k2, inner):
            lanes = pl.ds(pl.multiple_of(k2 * SIDE, SIDE), SIDE)
            for p in range(2):
                at = pl.ds(pl.multiple_of((p * coarse + k2) * CHUNK, CHUNK), CHUNK)
                xs[at, :] = x[p, rows, lanes].astype(F32)
            return inner

        lax.fori_loop(0, coarse, spread, 0, unroll=8)

        batch = 8

        def sweep_batch(step, inner):
            w1 = w1s[...]
            w2 = w2s[...]
            for j in range(0, batch, 2):
                at = [pl.ds(step * batch + j + h, 2 * coarse, stride=CHUNK) for h in range(2)]
                both = jnp.concatenate([xs[at[h], :].astype(BF16) for h in range(2)], axis=1)
                f = jnp.dot(w1, both, preferred_element_type=F32)
                turned = []
                for h in range(2):
                    part = f[:, h * SIDE:(h + 1) * SIDE]
                    re = jnp.concatenate([part[:coarse], part[:coarse]], axis=0)
                    im = jnp.concatenate([part[coarse:], part[coarse:]], axis=0)
                    cosine, sine = turn[0], turn[1]
                    turned.append(jnp.concatenate(
                        [(re * cosine - im * sine).astype(BF16), (re * sine + im * cosine).astype(BF16)], axis=1
                    ))
                y = lax.dot_general(
                    w2, jnp.concatenate(turned, axis=0), (((1,), (1,)), ((), ())), preferred_element_type=F32
                )
                for h in range(2):
                    ys[at[h], :] = y[:, h * SIDE:(h + 1) * SIDE]
            return inner

        lax.fori_loop(0, CHUNK // batch, sweep_batch, 0)

        def pack(band, inner):
            low = iota(CHUNK, SIDE, 1) < SIDE // 2
            piece, local = band // half, band % half
            for m in range(members):
                row = (m * bands + band) * CHUNK
                re = ys[pl.ds(pl.multiple_of(row, CHUNK), CHUNK), :]
                im = ys[pl.ds(pl.multiple_of(coarse * CHUNK + row, CHUNK), CHUNK), :]
                send0[m, q, band] = jnp.where(low, re, pltpu.roll(im, SIDE // 2, 1)).astype(BF16)
                send1[m, piece, q, local] = jnp.where(low, pltpu.roll(re, SIDE // 2, 1), im).astype(BF16)
            return inner

        lax.fori_loop(0, bands, pack, 0, unroll=2)
        for d in range(1, members):
            mem_copy(0, q, d).start()
        return carry

    lax.fori_loop(0, chunks, transform, 0)
    for piece in range(pieces):
        for d in range(1, members):
            mem_copy(1, piece, d).start()

    angle_copy.wait()
    factor = 1.0 / math.sqrt(all_sweeps)
    for a in range(tilts):
        c, s = cos_sin(angle[a * SIDE:(a + 1) * SIDE, :])
        lhs[a, 0] = (c * factor).astype(BF16)
        lhs[a, 1] = (s * factor).astype(BF16)

    blocks = slope_ref.shape[1]
    row_tab[...] = jnp.zeros_like(row_tab)
    row_tab[0:2, :blocks] = slope_ref[...]
    row_tab[2:3, :blocks] = owner_ref[...].astype(F32)

    def place(block):
        tilt, band = block // bands, block % bands
        return (band // 2) * (2 * tilts) + tilt * 2 + band % 2

    owner_row = row_tab[2:3, :]
    lane = iota(SIDE, SIDE, 1)
    taken = iota(SIDE, SIDE, 0)
    key = jnp.where(lane < blocks, jnp.broadcast_to(owner_row, (SIDE, SIDE)), (lane - blocks).astype(F32))
    limit = jnp.where(lane < blocks, place(lane), blocks)
    earlier = place(taken)
    follows = (key == down(owner_row)) & (taken < blocks) & (earlier < limit)
    chain = jnp.max(jnp.where(follows, earlier + 1, 0), axis=0, keepdims=True)
    chain_rows[...] = jnp.broadcast_to(chain, chain_rows.shape)
    chain_copy = pltpu.make_async_copy(chain_rows, chain_ref, chain_sem)
    chain_copy.start()

    part_lane = iota(SIDE, SIDE, 1)
    sign = jnp.where(part_lane < SIDE // 2, -1.0, 1.0)
    for h in range(2):
        across = (part_lane % (SIDE // 2) + h * (SIDE // 2)).astype(F32)
        c, s = cos_sin(across * down(row_tab[1:2, :]))
        for n, table in enumerate([c, s, sign * c, sign * s]):
            slant_tab[h, n] = table
    c, s = cos_sin(iota(SIDE, SIDE, 0).astype(F32) * row_tab[0:1, :])
    tilt_tab[0] = c
    tilt_tab[1] = s
    for d in range(2):
        stencils[d] = stencil(lead_ref[d:d + 1, :], weight_ref[d:d + 1, :])
    for h in range(2):
        sums[h, 0] = jnp.zeros((SIDE, SIDE), F32)

    recv0[me] = send0[me]
    recv1[me] = send1[me]

    def form(h, piece, i):
        n = piece * (half // 2) + i

        def band_rows(j):
            if h == 0:
                return [recv0[m, q, n * 2 + j] for m in range(members) for q in range(chunks)]
            return [recv1[m, piece, q, i * 2 + j] for m in range(members) for q in range(chunks)]

        rhs = jnp.concatenate([jnp.concatenate(band_rows(j), axis=0) for j in range(2)], axis=1)
        shift = (SIDE - n * 2) % SIDE
        cu = pltpu.roll(tilt_tab[0], shift, 1)
        su = pltpu.roll(tilt_tab[1], shift, 1)
        signs = jnp.where(iota(SIDE, SIDE, 1) < SIDE // 2, -1.0, 1.0)
        for a in range(tilts):
            with_cos = jnp.dot(lhs[a, 0], rhs, preferred_element_type=F32)
            with_sin = jnp.dot(lhs[a, 1], rhs, preferred_element_type=F32)
            for j in range(2):
                b = a * bands + n * 2 + j
                lanes = slice(j * SIDE, (j + 1) * SIDE)
                polar = with_cos[:, lanes] + signs * pltpu.roll(with_sin[:, lanes], SIDE // 2, 1)
                at = a * bands + j
                cb = cu[:, at:at + 1]
                sb = su[:, at:at + 1]
                cv, sv, signed_cv, signed_sv = [slant_tab[h, t, pl.ds(b, 1), :] for t in range(4)]
                cosine = cb * cv - sb * sv
                signed_sine = sb * signed_cv + cb * signed_sv
                demod = polar * cosine + pltpu.roll(polar, SIDE // 2, 1) * signed_sine
                sums[h, n * (2 * tilts) + a * 2 + j + 1] = sums[h, chain_ref[0, b]] + demod

    pairs = half // 2

    def form_piece(h, piece):
        def step(i, carry):
            form(h, piece, i)
            return carry

        lax.fori_loop(0, pairs, step, 0)

    def arrived(q, carry):
        for d in range(1, members):
            mem_copy(0, q, d).wait_recv()
        return carry

    def second_piece(piece, carry):
        for d in range(1, members):
            mem_copy(1, piece, d).wait_recv()
        form_piece(1, piece)
        return carry

    def tile_sum(h, o):
        return sums[h, chain_ref[0, blocks + o]]

    def pair_copy(h, d):
        return pltpu.make_async_remote_copy(
            src_ref=pair_out.at[h, d], dst_ref=pair_in.at[h, d],
            send_sem=pair_send.at[h, d], recv_sem=pair_recv.at[h, d],
            device_id=(partner, me), device_id_type=MESH,
        )

    def far_copy(h, d):
        to = (layer + d) % layers
        return pltpu.make_async_remote_copy(
            src_ref=far_out.at[h, d - 1], dst_ref=far_in.at[h, d - 1],
            send_sem=far_send.at[h, d - 1], recv_sem=far_recv.at[h, d - 1],
            device_id=(to * 2 + core, me), device_id_type=MESH,
        )

    order = list(range(1, layers)) + [0]

    def send_pair(h):
        for d in order:
            pair_out[h, d] = tile_sum(h, ((layer + d) % layers) * 2 + 1 - core).astype(BF16)
            pair_copy(h, d).start()

    def send_far(h):
        for d in range(1, layers):
            mine = tile_sum(h, ((layer + d) % layers) * 2 + core)
            pair_copy(h, d).wait_recv()
            far_out[h, d - 1] = (mine + pair_in[h, d].astype(F32)).astype(BF16)
            far_copy(h, d).start()
        pair_copy(h, 0).wait_recv()
        own[h] = tile_sum(h, layer * 2 + core) + pair_in[h, 0].astype(F32)

    chain_copy.wait()
    lax.fori_loop(0, chunks, arrived, 0)

    def first_step(n, carry):
        form(0, n // pairs, n % pairs)
        return carry

    lax.fori_loop(0, bands // 2, first_step, 0)
    send_pair(0)
    second_piece(0, 0)
    send_far(0)
    lax.fori_loop(1, pieces, second_piece, 0)
    send_pair(1)
    send_far(1)
    rows = []
    for h in range(2):
        for d in range(1, layers):
            far_copy(h, d).wait_recv()
            own[h] += far_in[h, d - 1].astype(F32)
        rows.append(jnp.dot(stencils[0], own[h].astype(BF16), preferred_element_type=F32))
    low = iota(SIDE, SIDE, 1) < SIDE // 2
    rows_done = jnp.concatenate(
        [
            jnp.where(low, rows[0], pltpu.roll(rows[1], SIDE // 2, 1)),
            jnp.where(low, pltpu.roll(rows[0], SIDE // 2, 1), rows[1]),
        ],
        axis=0,
    ).astype(BF16)
    tile = lax.dot_general(rows_done, stencils[1], (((1,), (1,)), ((), ())), preferred_element_type=F32)
    out_ref[...] = tile

    for h, count in ((0, chunks), (1, pieces)):
        def sent(n, carry, h=h):
            for d in range(1, members):
                mem_copy(h, n, d).wait_send()
            return carry

        lax.fori_loop(0, count, sent, 0)
        for d in order:
            pair_copy(h, d).wait_send()
        for d in range(1, layers):
            far_copy(h, d).wait_send()


def on_device(echo, angles, holder, slopes, lead, weight, *, groups, members):
    _, _, sweeps, frequencies = echo.shape
    _, _, angle_count, all_sweeps = angles.shape
    coarse = frequencies // SIDE
    bands = coarse // members
    pieces = min(4, bands // 2)
    half = bands // pieces
    chunks = sweeps // CHUNK
    tilts = angle_count // SIDE
    blocks = slopes.shape[3]
    layers = groups // 2
    exchange0 = (members, chunks, bands, CHUNK, SIDE)
    exchange1 = (members, pieces, chunks, half, CHUNK, SIDE)
    vmem = pl.BlockSpec(memory_space=pltpu.VMEM)
    anywhere = pl.BlockSpec(memory_space=pl.ANY)
    dma = pltpu.SemaphoreType.DMA
    tile = pl.pallas_call(
        functools.partial(kernel, groups, members),
        out_shape=jax.ShapeDtypeStruct((2 * SIDE, SIDE), F32),
        in_specs=[vmem, anywhere, anywhere, vmem, vmem, vmem],
        out_specs=vmem,
        scratch_shapes=[
            pltpu.VMEM((2, sweeps, frequencies), BF16),
            pltpu.VMEM((angle_count, all_sweeps), F32),
            pltpu.VMEM((2 * coarse * CHUNK, SIDE), F32),
            pltpu.VMEM((2 * coarse * CHUNK, SIDE), F32),
            pltpu.VMEM((2 * coarse, 2 * coarse), BF16),
            pltpu.VMEM((2 * coarse, 2 * SIDE), BF16),
            pltpu.VMEM((2, SIDE, SIDE), F32),
            pltpu.VMEM(exchange0, BF16),
            pltpu.VMEM(exchange0, BF16),
            pltpu.VMEM(exchange1, BF16),
            pltpu.VMEM(exchange1, BF16),
            pltpu.VMEM((tilts, 2, SIDE, all_sweeps), BF16),
            pltpu.VMEM((2, blocks + 1, SIDE, SIDE), F32),
            pltpu.VMEM((8, SIDE), F32),
            pltpu.VMEM((8, SIDE), I32),
            pltpu.SMEM((8, SIDE), I32),
            pltpu.VMEM((2, SIDE, SIDE), F32),
            pltpu.VMEM((2, 4, SIDE, SIDE), F32),
            pltpu.VMEM((2, SIDE, SIDE), BF16),
            pltpu.VMEM((2, layers, SIDE, SIDE), BF16),
            pltpu.VMEM((2, layers, SIDE, SIDE), BF16),
            pltpu.VMEM((2, layers - 1, SIDE, SIDE), BF16),
            pltpu.VMEM((2, layers - 1, SIDE, SIDE), BF16),
            pltpu.VMEM((2, SIDE, SIDE), F32),
            dma((chunks,)),
            dma,
            dma,
            dma((members - 1, chunks)),
            dma((members - 1, chunks)),
            dma((members - 1, pieces)),
            dma((members - 1, pieces)),
            dma((2, layers)),
            dma((2, layers)),
            dma((2, layers - 1)),
            dma((2, layers - 1)),
        ],
        compiler_params=pltpu.CompilerParams(
            vmem_limit_bytes=VMEM_LIMIT, collective_id=0, has_side_effects=True
        ),
    )(holder[0], echo[0], angles[0, 0], slopes[0, 0], lead[0, 0], weight[0, 0])
    return (0.25 * tile).astype(BF16).reshape(1, 2, SIDE, SIDE)


def solution(mesh):
    return jax.shard_map(
        functools.partial(on_device, groups=mesh.shape["sub"], members=mesh.shape["mem"]),
        mesh=mesh,
        in_specs=(
            P("sub", None, "mem", None),
            P("sub", "mem", None, None),
            P("sub", "mem", None),
            P("sub", "mem", None, None),
            P("sub", "mem", None, None),
            P("sub", "mem", None, None),
        ),
        out_specs=P(("sub", "mem"), None, None, None),
        check_vma=False,
    )
```

time: 43.7 us -> 43.6 us (level); the launches traced: 43.1 us -> 43.5 us
  no operation moved by 1% of the time
where the time goes in v5:
time: 43.6 us; the launch traced here: 43.5 us
  Pallas kernels  41.9 us (96%)
  other arithmetic  1.54 us (4%)
    pallas_call x1, Pallas kernels, on_device(): pl.pallas_call(functools.partial(kernel, groups, members), out_shape=jax....  41.9 us
    convert_element_type x1, other arithmetic, on_device(): return (0.25 * tile).astype(BF16).reshape(1, 2, SIDE, SIDE)  1.54 us

profile of v5, /device:TPU:0, one launch (start us, length us, event | category | flops | bytes accessed | tf_op | source)
XLA Modules:
  0.0 43.5 jit_solution(8258704899757785187)
XLA Ops:
  0.0 41.9 %shard_map.64 = f32[256,128]{1,0:T(8,128)} custom-call(s32[1,64]{1,0:T(1,128)} %bitcast.12, bf16[2,64,8192]{2,1,0:T(8,128)(2,1)} %bitcast.7, f32[512,256]{1,0:T(8,128)} %bitcast.8, f32[2,64]{1,0:T(2,128)} %bitcast.9, s32[2,128]{1,0:T(2,128)} %bitcast.10, f32[2,128]{1,0:T(2,128)} %bitcast.11), custom_call_target="tpu_custom_call" | custom-call | tf_op jit(solution)/shard_map/pallas_call | solution.py:377
  41.9 1.5 %multiply_convert_fusion = bf16[256,128]{1,0:T(8,128)(2,1)} fusion(f32[256,128]{1,0:T(8,128)} %shard_map.64), kind=kLoop, calls=%fused_computation | loop fusion | flops 65536 | bytes 196608 | tf_op jit(solution)/shard_map/convert_element_type | solution.py:423

commit v6 on v5

--- a/solution.py
+++ b/solution.py
@@ -110,19 +110,34 @@
     turn[1] = s * (1.0 / math.sqrt(frequencies))
 
     def mem_copy(h, n, d):
+        if h == 1:
+            return second_copy(n, d)
         to = (me + d) % members
-        src, dst = ((send0, recv0), (send1, recv1))[h]
-        send_sem, recv_sem = ((send_sem0, recv_sem0), (send_sem1, recv_sem1))[h]
         return pltpu.make_async_remote_copy(
-            src_ref=src.at[to, n],
-            dst_ref=dst.at[me, n],
-            send_sem=send_sem.at[d - 1, n],
-            recv_sem=recv_sem.at[d - 1, n],
+            src_ref=send0.at[to, n],
+            dst_ref=recv0.at[me, n],
+            send_sem=send_sem0.at[d - 1, n],
+            recv_sem=recv_sem0.at[d - 1, n],
             device_id=(sub, to),
             device_id_type=MESH,
         )
 
     pl.semaphore_wait(barrier, (members - 1) + 1 + (layers - 1))
+
+    ahead = 1 if chunks > 2 else 0
+
+    def second_copy(n, d):
+        to = (me + d) % members
+        part = (slice(None), slice(0, ahead)) if n is None else (n, slice(ahead, chunks))
+        slot = pieces if n is None else n
+        return pltpu.make_async_remote_copy(
+            src_ref=send1.at[(to,) + part],
+            dst_ref=recv1.at[(me,) + part],
+            send_sem=send_sem1.at[d - 1, slot],
+            recv_sem=recv_sem1.at[d - 1, slot],
+            device_id=(sub, to),
+            device_id_type=MESH,
+        )
 
     def transform(q, carry):
         x_copy(q).wait()
@@ -137,7 +152,7 @@
 
         lax.fori_loop(0, coarse, spread, 0, unroll=8)
 
-        batch = 8
+        batch = CHUNK
 
         def sweep_batch(step, inner):
             w1 = w1s[...]
@@ -180,7 +195,11 @@
             mem_copy(0, q, d).start()
         return carry
 
-    lax.fori_loop(0, chunks, transform, 0)
+    if ahead:
+        lax.fori_loop(0, ahead + 1, transform, 0)
+        for d in range(1, members):
+            second_copy(None, d).start()
+    lax.fori_loop(ahead + 1 if ahead else 0, chunks, transform, 0)
     for piece in range(pieces):
         for d in range(1, members):
             mem_copy(1, piece, d).start()
@@ -323,6 +342,9 @@
 
     lax.fori_loop(0, bands // 2, first_step, 0)
     send_pair(0)
+    if ahead:
+        for d in range(1, members):
+            second_copy(None, d).wait_recv()
     second_piece(0, 0)
     send_far(0)
     lax.fori_loop(1, pieces, second_piece, 0)
@@ -345,6 +367,9 @@
     tile = lax.dot_general(rows_done, stencils[1], (((1,), (1,)), ((), ())), preferred_element_type=F32)
     out_ref[...] = tile
 
+    if ahead:
+        for d in range(1, members):
+            second_copy(None, d).wait_send()
     for h, count in ((0, chunks), (1, pieces)):
         def sent(n, carry, h=h):
             for d in range(1, members):
@@ -409,8 +434,8 @@
             dma,
             dma((members - 1, chunks)),
             dma((members - 1, chunks)),
-            dma((members - 1, pieces)),
-            dma((members - 1, pieces)),
+            dma((members - 1, pieces + 1)),
+            dma((members - 1, pieces + 1)),
             dma((2, layers)),
             dma((2, layers)),
             dma((2, layers - 1)),

time: 43.6 us -> 46.5 us (1.067)
  Pallas kernels: 41.9 us -> 44.8 us
    pallas_call x1, Pallas kernels: 41.9 us -> 44.8 us  [on_device(): pl.pallas_call(functools.partial(kernel, groups, members), out_shape=jax....]
where the time goes in v6:
time: 46.5 us; the launch traced here: 46.4 us
  Pallas kernels  44.8 us (96%)
  other arithmetic  1.54 us (3%)
    pallas_call x1, Pallas kernels, on_device(): pl.pallas_call(functools.partial(kernel, groups, members), out_shape=jax....  44.8 us
    convert_element_type x1, other arithmetic, on_device(): return (0.25 * tile).astype(BF16).reshape(1, 2, SIDE, SIDE)  1.54 us

profile of v6, /device:TPU:0, one launch (start us, length us, event | category | flops | bytes accessed | tf_op | source)
XLA Modules:
  0.0 46.4 jit_solution(5635946882897915400)
XLA Ops:
  0.0 44.8 %shard_map.64 = f32[256,128]{1,0:T(8,128)} custom-call(s32[1,64]{1,0:T(1,128)} %bitcast.12, bf16[2,64,8192]{2,1,0:T(8,128)(2,1)} %bitcast.7, f32[512,256]{1,0:T(8,128)} %bitcast.8, f32[2,64]{1,0:T(2,128)} %bitcast.9, s32[2,128]{1,0:T(2,128)} %bitcast.10, f32[2,128]{1,0:T(2,128)} %bitcast.11), custom_call_target="tpu_custom_call" | custom-call | tf_op jit(solution)/shard_map/pallas_call | solution.py:402
  44.8 1.5 %multiply_convert_fusion = bf16[256,128]{1,0:T(8,128)(2,1)} fusion(f32[256,128]{1,0:T(8,128)} %shard_map.64), kind=kLoop, calls=%fused_computation | loop fusion | flops 65536 | bytes 196608 | tf_op jit(solution)/shard_map/convert_element_type | solution.py:448

commit v7 on v5

--- a/solution.py
+++ b/solution.py
@@ -68,7 +68,7 @@
 def kernel(
     groups, members,
     owner_ref, x_hbm, angle_hbm, slope_ref, lead_ref, weight_ref, out_ref,
-    x, angle, xs, ys, w1s, w2s, turn, send0, recv0, send1, recv1, lhs, sums, row_tab, chain_rows, chain_ref, tilt_tab, slant_tab, stencils,
+    x, angle, xs, ys, w1s, w2s, turn, send0, recv0, send1, recv1, lhs, product, sums, row_tab, chain_rows, chain_ref, tilt_tab, slant_tab, stencils,
     pair_out, pair_in, far_out, far_in, own,
     x_sem, angle_sem, chain_sem, send_sem0, recv_sem0, send_sem1, recv_sem1, pair_send, pair_recv, far_send, far_recv,
 ):
@@ -189,8 +189,8 @@
     factor = 1.0 / math.sqrt(all_sweeps)
     for a in range(tilts):
         c, s = cos_sin(angle[a * SIDE:(a + 1) * SIDE, :])
-        lhs[a, 0] = (c * factor).astype(BF16)
-        lhs[a, 1] = (s * factor).astype(BF16)
+        lhs[2 * a * SIDE:(2 * a + 1) * SIDE, :] = (c * factor).astype(BF16)
+        lhs[(2 * a + 1) * SIDE:(2 * a + 2) * SIDE, :] = (s * factor).astype(BF16)
 
     blocks = slope_ref.shape[1]
     row_tab[...] = jnp.zeros_like(row_tab)
@@ -244,13 +244,14 @@
         cu = pltpu.roll(tilt_tab[0], shift, 1)
         su = pltpu.roll(tilt_tab[1], shift, 1)
         signs = jnp.where(iota(SIDE, SIDE, 1) < SIDE // 2, -1.0, 1.0)
+        product[...] = jnp.dot(lhs[...], rhs, preferred_element_type=F32)
         for a in range(tilts):
-            with_cos = jnp.dot(lhs[a, 0], rhs, preferred_element_type=F32)
-            with_sin = jnp.dot(lhs[a, 1], rhs, preferred_element_type=F32)
             for j in range(2):
                 b = a * bands + n * 2 + j
                 lanes = slice(j * SIDE, (j + 1) * SIDE)
-                polar = with_cos[:, lanes] + signs * pltpu.roll(with_sin[:, lanes], SIDE // 2, 1)
+                with_cos = product[2 * a * SIDE:(2 * a + 1) * SIDE, lanes]
+                with_sin = product[(2 * a + 1) * SIDE:(2 * a + 2) * SIDE, lanes]
+                polar = with_cos + signs * pltpu.roll(with_sin, SIDE // 2, 1)
                 at = a * bands + j
                 cb = cu[:, at:at + 1]
                 sb = su[:, at:at + 1]
@@ -391,7 +392,8 @@
             pltpu.VMEM(exchange0, BF16),
             pltpu.VMEM(exchange1, BF16),
             pltpu.VMEM(exchange1, BF16),
-            pltpu.VMEM((tilts, 2, SIDE, all_sweeps), BF16),
+            pltpu.VMEM((2 * angle_count, all_sweeps), BF16),
+            pltpu.VMEM((2 * angle_count, 2 * SIDE), F32),
             pltpu.VMEM((2, blocks + 1, SIDE, SIDE), F32),
             pltpu.VMEM((8, SIDE), F32),
             pltpu.VMEM((8, SIDE), I32),

time: 43.6 us -> 43.6 us (level)
  no operation moved by 1% of the time
where the time goes in v7:
time: 43.6 us; the launch traced here: 43.4 us
  Pallas kernels  41.9 us (96%)
  other arithmetic  1.54 us (4%)
    pallas_call x1, Pallas kernels, on_device(): pl.pallas_call(functools.partial(kernel, groups, members), out_shape=jax....  41.9 us
    convert_element_type x1, other arithmetic, on_device(): return (0.25 * tile).astype(BF16).reshape(1, 2, SIDE, SIDE)  1.54 us

profile of v7, /device:TPU:0, one launch (start us, length us, event | category | flops | bytes accessed | tf_op | source)
XLA Modules:
  0.0 43.4 jit_solution(6474306608688307098)
XLA Ops:
  0.0 41.9 %shard_map.64 = f32[256,128]{1,0:T(8,128)} custom-call(s32[1,64]{1,0:T(1,128)} %bitcast.12, bf16[2,64,8192]{2,1,0:T(8,128)(2,1)} %bitcast.7, f32[512,256]{1,0:T(8,128)} %bitcast.8, f32[2,64]{1,0:T(2,128)} %bitcast.9, s32[2,128]{1,0:T(2,128)} %bitcast.10, f32[2,128]{1,0:T(2,128)} %bitcast.11), custom_call_target="tpu_custom_call" | custom-call | tf_op jit(solution)/shard_map/pallas_call | solution.py:378
  41.9 1.5 %multiply_convert_fusion = bf16[256,128]{1,0:T(8,128)(2,1)} fusion(f32[256,128]{1,0:T(8,128)} %shard_map.64), kind=kLoop, calls=%fused_computation | loop fusion | flops 65536 | bytes 196608 | tf_op jit(solution)/shard_map/convert_element_type | solution.py:425

commit v8 on v7

--- a/solution.py
+++ b/solution.py
@@ -137,7 +137,7 @@
 
         lax.fori_loop(0, coarse, spread, 0, unroll=8)
 
-        batch = 8
+        batch = 4
 
         def sweep_batch(step, inner):
             w1 = w1s[...]
@@ -383,8 +383,8 @@
         scratch_shapes=[
             pltpu.VMEM((2, sweeps, frequencies), BF16),
             pltpu.VMEM((angle_count, all_sweeps), F32),
-            pltpu.VMEM((2 * coarse * CHUNK, SIDE), F32),
-            pltpu.VMEM((2 * coarse * CHUNK, SIDE), F32),
+            pltpu.VMEM(((2 * coarse + 1) * CHUNK, SIDE), F32),
+            pltpu.VMEM(((2 * coarse + 1) * CHUNK, SIDE), F32),
             pltpu.VMEM((2 * coarse, 2 * coarse), BF16),
             pltpu.VMEM((2 * coarse, 2 * SIDE), BF16),
             pltpu.VMEM((2, SIDE, SIDE), F32),

time: 43.6 us -> 45 us (1.032)
  Pallas kernels: 41.9 us -> 43.3 us
    pallas_call x1, Pallas kernels: 41.9 us -> 43.3 us  [on_device(): pl.pallas_call(functools.partial(kernel, groups, members), out_shape=jax....]
where the time goes in v8:
time: 45 us; the launch traced here: 44.8 us
  Pallas kernels  43.3 us (96%)
  other arithmetic  1.54 us (3%)
    pallas_call x1, Pallas kernels, on_device(): pl.pallas_call(functools.partial(kernel, groups, members), out_shape=jax....  43.3 us
    convert_element_type x1, other arithmetic, on_device(): return (0.25 * tile).astype(BF16).reshape(1, 2, SIDE, SIDE)  1.54 us

profile of v8, /device:TPU:0, one launch (start us, length us, event | category | flops | bytes accessed | tf_op | source)
XLA Modules:
  0.0 44.8 jit_solution(5232164290664726702)
XLA Ops:
  0.0 43.3 %shard_map.64 = f32[256,128]{1,0:T(8,128)} custom-call(s32[1,64]{1,0:T(1,128)} %bitcast.12, bf16[2,64,8192]{2,1,0:T(8,128)(2,1)} %bitcast.7, f32[512,256]{1,0:T(8,128)} %bitcast.8, f32[2,64]{1,0:T(2,128)} %bitcast.9, s32[2,128]{1,0:T(2,128)} %bitcast.10, f32[2,128]{1,0:T(2,128)} %bitcast.11), custom_call_target="tpu_custom_call" | custom-call | tf_op jit(solution)/shard_map/pallas_call | solution.py:378
  43.3 1.5 %multiply_convert_fusion = bf16[256,128]{1,0:T(8,128)(2,1)} fusion(f32[256,128]{1,0:T(8,128)} %shard_map.64), kind=kLoop, calls=%fused_computation | loop fusion | flops 65536 | bytes 196608 | tf_op jit(solution)/shard_map/convert_element_type | solution.py:425
